TPU v7x, 256 devices: a whole 4x4x8 slice. The times are simulated.
256 devices in a mesh: dp: 64 (over z, y, core), head: 4 (over x).
Axes of the slice: x: 4, y: 4, z: 8, core: 2. Of those that a mesh axis runs over, the one named last changes fastest.
Arguments:
- queries: bfloat16 [16384, 8192], P('dp', 'head'), may hold values from -128 to 128
- answer_keys: bfloat16 [16384, 1024], P('dp', 'head'), may hold values from -5 to 5
- answer_values: bfloat16 [16384, 1024], P('dp', 'head'), may hold values from -6 to 6
- prompt_keys: bfloat16 [64, 256, 1024], P('dp', 'head'), may hold values from -6 to 6
- prompt_values: bfloat16 [64, 256, 1024], P('dp', 'head'), may hold values from -6 to 6
- output_gradient: bfloat16 [16384, 8192], P('dp', 'head'), may hold values from -6 to 6
- prompt_len: int32 [64], replicated, may hold values from 64 to 256
- response_len: int32 [256], P('dp'), may hold values from 1 to 64
- response_prompt: int32 [256], P('dp'), may hold values from 0 to 63, as said below
Outputs:
- attended: bfloat16 [16384, 8192], P('dp', 'head')
- grad_query: bfloat16 [16384, 8192], P('dp', 'head')
- grad_response_keys: bfloat16 [16384, 1024], P('dp', 'head')
- grad_response_values: bfloat16 [16384, 1024], P('dp', 'head')
- grad_prompt_keys: float32 [64, 256, 1024], P('dp', 'head')
- grad_prompt_values: float32 [64, 256, 1024], P('dp', 'head')
Inputs may be any that keep to these rules, and one draw needn't show every extreme that they name: `response_prompt`: prompt p is the one at dp index p; the prompt of a slot at dp index i lies at most 2 indices from i, counted cyclically over 64, and both distances 2 occur.
All inputs are finite; a program needn't handle non-finite values.
Results may differ from a plain program's by a relative error of at most 0.035.
Values may be sent and summed in bfloat16 or wider, within the bound.
A program may use at most 64 MiB of HBM per device.

v0:
```python
import math

import jax
import jax.numpy as jnp
from jax import lax
from jax.sharding import PartitionSpec as P

HEAD_SIZE = 128
PLEN = 256
MAX_SPREAD = 2


def passed_along(x, axis, by):
    size = lax.axis_size(axis)
    return lax.ppermute(x, axis, [(i, (i + by) % size) for i in range(size)])


def for_sending(x):

    def short(part):
        return part.astype(jnp.bfloat16) if part.dtype == jnp.float32 else part

    return jax.tree.map(short, x)


def on_device(
    queries,
    answer_keys,
    answer_values,
    prompt_keys,
    prompt_values,
    output_gradient,
    prompt_len,
    response_len,
    response_prompt,
):
    slots = response_len.shape[0]
    answer_rows = queries.shape[0] // slots
    local_kv = answer_keys.shape[1] // HEAD_SIZE
    group_width = queries.shape[1] // HEAD_SIZE // local_kv
    columns = local_kv * HEAD_SIZE
    devices = lax.axis_size("dp")
    own_index = lax.axis_index("dp")
    stacked = jnp.concatenate([prompt_keys, prompt_values], axis=0)
    key_value = lax.all_to_all(stacked, "head", split_axis=2, concat_axis=1, tiled=True)
    neighbours = {0: key_value}
    for offset in range(-MAX_SPREAD, MAX_SPREAD + 1):
        if offset != 0:
            neighbours[offset] = passed_along(key_value, "dp", -offset)
    relative = jnp.mod(response_prompt - own_index, devices)
    relative = jnp.where(relative > devices // 2, relative - devices, relative)
    prompt_size = jnp.take(prompt_len, response_prompt)
    chosen = jnp.broadcast_to(neighbours[0][None], (slots,) + neighbours[0].shape)
    for offset in range(-MAX_SPREAD, MAX_SPREAD + 1):
        if offset != 0:
            pick = (relative == offset)[:, None, None, None]
            chosen = jnp.where(pick, neighbours[offset][None], chosen)
    head_keys = chosen[:, 0].reshape(slots, PLEN, local_kv, HEAD_SIZE)
    head_values = chosen[:, 1].reshape(slots, PLEN, local_kv, HEAD_SIZE)
    tail_keys = answer_keys.reshape(slots, answer_rows, local_kv, HEAD_SIZE)
    tail_values = answer_values.reshape(slots, answer_rows, local_kv, HEAD_SIZE)
    slot_query = queries.reshape(slots, answer_rows, local_kv, group_width, HEAD_SIZE)
    scaling = 1.0 / math.sqrt(HEAD_SIZE)
    head_scores = (
        jnp.einsum("ntkgd,njkd->nkgtj", slot_query, head_keys, preferred_element_type=jnp.float32)
        * scaling
    )
    tail_scores = (
        jnp.einsum("ntkgd,njkd->nkgtj", slot_query, tail_keys, preferred_element_type=jnp.float32)
        * scaling
    )
    head_cols = jnp.arange(PLEN, dtype=jnp.int32)
    head_seen = (head_cols[None, :] < prompt_size[:, None])[:, None, None, None, :]
    rows_at = jnp.arange(answer_rows, dtype=jnp.int32)
    tail_seen = (rows_at[None, :] <= rows_at[:, None])[None, None, None]
    head_max = jnp.max(jnp.where(head_seen, head_scores, -jnp.inf), axis=-1, keepdims=True)
    tail_max = jnp.max(jnp.where(tail_seen, tail_scores, -jnp.inf), axis=-1, keepdims=True)
    row_max = jnp.maximum(head_max, tail_max)
    head_exp = jnp.where(head_seen, jnp.exp(head_scores - row_max), 0.0)
    tail_exp = jnp.where(tail_seen, jnp.exp(tail_scores - row_max), 0.0)
    total = jnp.sum(head_exp, axis=-1, keepdims=True) + jnp.sum(tail_exp, axis=-1, keepdims=True)
    head_prob = head_exp / total
    tail_prob = tail_exp / total
    head_weights = head_prob.astype(jnp.bfloat16)
    tail_weights = tail_prob.astype(jnp.bfloat16)
    live_rows = rows_at[None, :] < response_len[:, None]
    live_scale = live_rows.astype(jnp.float32)[:, :, None, None, None]
    mixed = jnp.einsum(
        "nkgtj,njkd->ntkgd", head_weights, head_values, preferred_element_type=jnp.float32
    )
    mixed = mixed + jnp.einsum(
        "nkgtj,njkd->ntkgd", tail_weights, tail_values, preferred_element_type=jnp.float32
    )
    attended = (mixed * live_scale).astype(jnp.bfloat16)
    grad_live = (
        output_gradient.reshape(slots, answer_rows, local_kv, group_width, HEAD_SIZE)
        * live_rows.astype(jnp.bfloat16)[:, :, None, None, None]
    )
    row_delta = jnp.einsum(
        "ntkgd,ntkgd->nkgt", grad_live, attended, preferred_element_type=jnp.float32
    )[..., None]
    head_gvalues = jnp.einsum(
        "nkgtj,ntkgd->njkd", head_weights, grad_live, preferred_element_type=jnp.float32
    )
    tail_gvalues = jnp.einsum(
        "nkgtj,ntkgd->njkd", tail_weights, grad_live, preferred_element_type=jnp.float32
    )
    head_gprobs = jnp.einsum(
        "ntkgd,njkd->nkgtj", grad_live, head_values, preferred_element_type=jnp.float32
    )
    tail_gprobs = jnp.einsum(
        "ntkgd,njkd->nkgtj", grad_live, tail_values, preferred_element_type=jnp.float32
    )
    head_gscores = (head_prob * (head_gprobs - row_delta)).astype(jnp.bfloat16)
    tail_gscores = (tail_prob * (tail_gprobs - row_delta)).astype(jnp.bfloat16)
    query_sum = jnp.einsum(
        "nkgtj,njkd->ntkgd", head_gscores, head_keys, preferred_element_type=jnp.float32
    )
    query_sum = query_sum + jnp.einsum(
        "nkgtj,njkd->ntkgd", tail_gscores, tail_keys, preferred_element_type=jnp.float32
    )
    grad_query = (query_sum * scaling).astype(jnp.bfloat16)
    head_gkeys = (
        jnp.einsum(
            "nkgtj,ntkgd->njkd", head_gscores, slot_query, preferred_element_type=jnp.float32
        )
        * scaling
    )
    tail_gkeys = (
        jnp.einsum(
            "nkgtj,ntkgd->njkd", tail_gscores, slot_query, preferred_element_type=jnp.float32
        )
        * scaling
    )
    offsets = jnp.arange(-MAX_SPREAD, MAX_SPREAD + 1, dtype=jnp.int32)
    selector = (offsets[:, None] == relative[None, :]).astype(jnp.float32)
    key_part = jnp.einsum(
        "ws,spc->wpc",
        selector,
        head_gkeys.reshape(slots, PLEN, columns),
        precision=lax.Precision.HIGHEST,
    )
    value_part = jnp.einsum(
        "ws,spc->wpc",
        selector,
        head_gvalues.reshape(slots, PLEN, columns),
        precision=lax.Precision.HIGHEST,
    )
    partial_value = jnp.stack([key_part, value_part], axis=1)
    summed = partial_value[MAX_SPREAD]
    for offset in range(-MAX_SPREAD, MAX_SPREAD + 1):
        if offset != 0:
            summed = summed + passed_along(
                partial_value[offset + MAX_SPREAD].astype(jnp.bfloat16), "dp", offset
            ).astype(jnp.float32)
    returned = lax.all_to_all(
        for_sending(summed), "head", split_axis=1, concat_axis=2, tiled=True
    ).astype(summed.dtype)
    token_rows = slots * answer_rows
    return (
        attended.reshape(token_rows, -1),
        grad_query.reshape(token_rows, -1),
        tail_gkeys.reshape(token_rows, columns).astype(jnp.bfloat16),
        tail_gvalues.reshape(token_rows, columns).astype(jnp.bfloat16),
        returned[0:1],
        returned[1:2],
    )


def solution(mesh):
    in_specs = (
        P("dp", "head"),
        P("dp", "head"),
        P("dp", "head"),
        P("dp", "head", None),
        P("dp", "head", None),
        P("dp", "head"),
        P(),
        P("dp"),
        P("dp"),
    )
    out_specs = (
        P("dp", "head"),
        P("dp", "head"),
        P("dp", "head"),
        P("dp", "head"),
        P("dp", "head", None),
        P("dp", "head", None),
    )
    return jax.shard_map(
        on_device, mesh=mesh, in_specs=in_specs, out_specs=out_specs, check_vma=False
    )
```

profile of v0, /device:TPU:1, one launch (start us, length us, event | category | flops | bytes accessed | tf_op | source)
XLA Modules:
  0.0 106.4 jit_solution(3566645164733267343)
XLA Ops:
  3.3 4.8 %all-to-all-start = ((bf16[4,2,16384]{2,1,0:T(2,128)(2,1)}), bf16[4,2,16384]{2,1,0:T(2,128)(2,1)S(1)}, u32[]{:S(2)}, u32[]{:S(2)}) async-start(bf16[4,2,16384]{2,1,0:T(2,128)(2,1)} %reshape.188), calls=%async_computation | async-start | bytes 524288 | tf_op jit(solution)/shard_map/all_to_all | solution.py:45
  10.8 1.8 %fusion.15 = (f32[4,2,8,64]{3,2,1,0:T(8,128)}, f32[4,2,64,64,8]{3,2,4,1,0:T(8,128)S(1)}) fusion(pred[64,64]{0,1:T(8,128)(4,1)S(1)} %iota_compare_fusion, bf16[4,64,2,8,128]{4,3,2,1,0:T(8,128)(2,1)S(1)} %bitcast.194, bf16[4,64,2,128,1]{3,2,1,0,4:T(2,128)(2,1)S(1)} %bitcast.203), kind=kOutput, calls=%fused_computation.28 | convolution fusion | flops 67891200 | bytes 2248704 | tf_op jit(solution)/shard_map/ntkgd,njkd->nkgtj/dot_general | solution.py:69
  14.8 1.5 %copy.250 = bf16[2,64,4,256]{3,2,1,0:T(4,128)(2,1)S(1)} copy(bf16[2,64,4,256]{1,0,3,2:T(2,128)(2,1)} %bitcast.202) | data formatting | bytes 524288 | tf_op jit(solution)/shard_map/all_to_all | solution.py:45
  17.0 1.3 %collective-permute-start.3 = (bf16[2,256,256]{2,1,0:T(8,128)(2,1)}, bf16[2,256,256]{2,1,0:T(8,128)(2,1)}, u32[]{:S(2)}, u32[]{:S(2)}) collective-permute-start(bf16[2,256,256]{2,1,0:T(8,128)(2,1)} %bitcast.4), channel_id=1, source_target_pairs={{0,8},{4,12},{8,16},{12,20},{16,24},{20,28},{24,32},{28,36},{32,40... | collective-permute-start | bytes 786440 | tf_op jit(solution)/shard_map/ppermute | solution.py:15
  18.3 3.5 %collective-permute-start.2 = (bf16[2,256,256]{2,1,0:T(8,128)(2,1)}, bf16[2,256,256]{2,1,0:T(8,128)(2,1)}, u32[]{:S(2)}, u32[]{:S(2)}) collective-permute-start(bf16[2,256,256]{2,1,0:T(8,128)(2,1)} %bitcast.4), channel_id=1, source_target_pairs={{0,4},{4,8},{8,12},{12,16},{16,20},{20,24},{24,28},{28,32},{32,36}... | collective-permute-start | bytes 786440 | tf_op jit(solution)/shard_map/ppermute | solution.py:15
  21.9 5.3 %collective-permute-start = (bf16[2,256,256]{2,1,0:T(8,128)(2,1)}, bf16[2,256,256]{2,1,0:T(8,128)(2,1)}, u32[]{:S(2)}, u32[]{:S(2)}) collective-permute-start(bf16[2,256,256]{2,1,0:T(8,128)(2,1)} %bitcast.4), channel_id=1, source_target_pairs={{0,248},{4,252},{8,0},{12,4},{16,8},{20,12},{24,16},{28,20},{32,24... | collective-permute-start | bytes 786440 | tf_op jit(solution)/shard_map/ppermute | solution.py:15
  27.7 1.6 %reshape.156 = bf16[4,64,2,128]{3,2,1,0:T(2,128)(2,1)} reshape(bf16[256,256]{1,0:T(8,128)(2,1)} %param.11) | data formatting | bytes 262144 | tf_op jit(solution)/shard_map/reshape | solution.py:61
  29.3 2.4 %copy.274 = bf16[32,8,16,128]{3,2,1,0:T(8,128)(2,1)} copy(bf16[32,8,16,128]{3,1,2,0:T(8,128)(2,1)} %bitcast.208) | data formatting | bytes 2097152
  34.1 1.8 %copy.202 = bf16[2,256,256]{1,2,0:T(8,128)(2,1)} copy(bf16[2,256,256]{2,1,0:T(8,128)(2,1)} %collective-permute-done.3) | data formatting | bytes 524288 | tf_op jit(solution)/shard_map/ppermute | solution.py:15
  35.9 1.8 %copy.201 = bf16[2,256,256]{1,2,0:T(8,128)(2,1)} copy(bf16[2,256,256]{2,1,0:T(8,128)(2,1)} %collective-permute-done.2) | data formatting | bytes 524288 | tf_op jit(solution)/shard_map/ppermute | solution.py:15
  37.7 1.8 %copy.200 = bf16[2,256,256]{1,2,0:T(8,128)(2,1)} copy(bf16[2,256,256]{2,1,0:T(8,128)(2,1)} %collective-permute-done.1) | data formatting | bytes 524288 | tf_op jit(solution)/shard_map/ppermute | solution.py:15
  39.5 1.8 %copy.199 = bf16[2,256,256]{1,2,0:T(8,128)(2,1)} copy(bf16[2,256,256]{2,1,0:T(8,128)(2,1)} %collective-permute-done) | data formatting | bytes 524288 | tf_op jit(solution)/shard_map/ppermute | solution.py:15
  41.3 1.5 %select_select_fusion = bf16[4,2,256,256]{2,3,0,1:T(8,128)(2,1)S(1)} fusion(pred[4]{0:T(512)(128)(4,1)} %get-tuple-element.19, pred[4]{0:T(512)(128)(4,1)} %get-tuple-element.20, pred[4]{0:T(512)(128)(4,1)} %get-tuple-element.18, pred[4]{0:T(512)(128)(4,1)} %get-tuple-element.6, bf16[2,256,256]{1,2,0:T(8,128)(2,1)S(1)} %copy.203, ...), kind=kLoop, calls=%fused_computation.49 | loop fusion | flops 2097152 | bytes 2359312 | tf_op jit(solution)/shard_map/jit(_where)/select_n | solution.py:57
  44.5 1.7 %fusion.7 = f32[4,2,8,64]{3,2,1,0:T(8,128)S(1)} fusion(f32[4,2,256,64,8]{2,3,4,1,0:T(8,128)S(1)} %get-tuple-element.22, f32[4,2,8,64]{3,2,1,0:T(8,128)S(1)} %max.8, pred[4,256]{1,0:T(4,128)(4,1)S(1)} %copy-done.13), kind=kLoop, calls=%fused_computation.14 | loop fusion | flops 4190208 | bytes 4228096 | tf_op jit(solution)/shard_map/reduce_sum | solution.py:81
  46.2 1.6 %fusion.25 = bf16[4,64,2,128]{3,1,2,0:T(8,128)(2,1)} fusion(bf16[4,64,2,8,128]{4,3,2,1,0:T(8,128)(2,1)S(1)} %bitcast.209, bf16[4,64]{1,0:T(4,128)(2,1)S(1)} %copy-done.16, f32[4,2,64,64,8]{3,2,4,1,0:T(8,128)S(1)} %get-tuple-element.24, f32[4,2,8,64]{3,2,1,0:T(8,128)S(1)} %add.46, f32[4,2,8,64]{3,2,1,0:T(8,128)S(1)} %max.8, ...), kind=kOutput, calls=%fused_computation.43 | convolution fusion | flops 70582272 | bytes 2265600 | tf_op jit(solution)/shard_map/nkgtj,ntkgd->njkd/dot_general | solution.py:105
  47.7 3.3 %fusion.26 = f32[4,2,128,256,1]{3,2,4,1,0:T(8,128)} fusion(bf16[4,64,2,8,128]{4,3,2,1,0:T(8,128)(2,1)S(1)} %bitcast.210, bf16[4,64]{1,0:T(4,128)(2,1)S(1)} %copy-done.16, f32[4,2,256,64,8]{2,3,4,1,0:T(8,128)S(1)} %get-tuple-element.22, f32[4,2,8,64]{3,2,1,0:T(8,128)S(1)} %add.46, f32[4,2,8,64]{3,2,1,0:T(8,128)S(1)} %max.8, pred[4,256]{1,0:T(4,128)(4,1)S(1)} %copy-done.13), kind=kOutput, calls=%fused_computation.45 | convolution fusion | flops 274202624 | bytes 6325760 | tf_op jit(solution)/shard_map/nkgtj,ntkgd->njkd/dot_general | solution.py:102
  51.1 1.9 %fusion.28 = f32[4,2,128,8,64]{2,4,3,1,0:T(8,128)S(1)} fusion(bf16[4,256,2,128,1]{1,3,4,2,0:T(8,128)(2,1)S(1)} %bitcast.217, f32[4,2,256,64,8]{2,3,4,1,0:T(8,128)S(1)} %get-tuple-element.22, f32[4,2,8,64]{3,2,1,0:T(8,128)S(1)} %add.46, f32[4,2,8,64]{3,2,1,0:T(8,128)S(1)} %max.8, pred[4,256]{1,0:T(4,128)(4,1)S(1)} %copy-done.13), kind=kOutput, calls=%fused_computation.47 | convolution fusion | flops 273678336 | bytes 6849536 | tf_op jit(solution)/shard_map/nkgtj,njkd->ntkgd/dot_general | solution.py:88
  53.0 2.2 %fusion.12 = (f32[4,2,8,64]{3,2,1,0:T(8,128)S(1)}, bf16[4,64,2,8,128]{4,1,3,2,0:T(8,128)(2,1)}) fusion(bf16[4,64]{1,0:T(4,128)(2,1)S(1)} %copy-done.16, bf16[4,64,2,8,128]{4,3,2,1,0:T(8,128)(2,1)S(1)} %bitcast.211, f32[4,64]{1,0:T(4,128)S(1)} %copy-done.15, bf16[4,64,2,128,1]{3,2,1,0,4:T(2,128)(2,1)S(1)} %bitcast.220, f32[4,2,8,64]{3,2,1,0:T(8,128)S(1)} %add.46, ...), kind=kOutput, calls=%fused_computation.22 | convolution fusion | flops 72609792 | bytes 5428736 | tf_op jit(solution)/shard_map/nkgtj,njkd->ntkgd/dot_general | solution.py:91
  55.2 2.4 %fusion.2 = bf16[4,2,8,64,256]{4,3,2,1,0:T(8,128)(2,1)S(1)} fusion(bf16[4,256,2,128,1]{1,3,4,2,0:T(8,128)(2,1)S(1)} %bitcast.218, f32[4,2,8,64]{3,2,1,0:T(8,128)S(1)} %get-tuple-element.25, bf16[4,64,2,8,128]{4,3,2,1,0:T(8,128)(2,1)S(1)} %bitcast.212, bf16[4,64]{1,0:T(4,128)(2,1)S(1)} %copy-done.16, f32[4,2,8,64]{3,2,1,0:T(8,128)S(1)} %add.46, ...), kind=kOutput, calls=%fused_computation.7 | convolution fusion | flops 277872640 | bytes 7915008 | tf_op jit(solution)/shard_map/ntkgd,njkd->nkgtj/dot_general | solution.py:108
  57.6 2.2 %fusion.11 = bf16[4,2,8,64,64]{3,4,2,1,0:T(8,128)(2,1)} fusion(f32[4,2,8,64]{3,2,1,0:T(8,128)S(1)} %get-tuple-element.25, bf16[4,64,2,128,1]{3,2,1,0,4:T(2,128)(2,1)S(1)} %bitcast.221, bf16[4,64,2,8,128]{4,3,2,1,0:T(8,128)(2,1)S(1)} %bitcast.213, bf16[4,64]{1,0:T(4,128)(2,1)S(1)} %copy-done.16, f32[4,2,8,64]{3,2,1,0:T(8,128)S(1)} %add.46, ...), kind=kOutput, calls=%fused_computation.20 | convolution fusion | flops 69468160 | bytes 2806272 | tf_op jit(solution)/shard_map/ntkgd,njkd->nkgtj/dot_general | solution.py:111
  60.4 2.0 %fusion.65 = f32[4,2,128,8,64]{2,4,3,1,0:T(8,128)} fusion(bf16[4,256,2,128,1]{1,3,4,2,0:T(8,128)(2,1)S(1)} %bitcast.199, bf16[4,2,8,64,256]{4,3,2,1,0:T(8,128)(2,1)S(1)} %fusion.2), kind=kOutput, calls=%fused_computation.105 | convolution fusion | flops 268435456 | bytes 4718592 | tf_op jit(solution)/shard_map/nkgtj,njkd->ntkgd/dot_general | solution.py:116
  65.1 2.7 %convolution_bitcast_fusion = f32[5,1,256,256]{3,0,2,1:T(8,128)S(1)} fusion(f32[4,256,256]{2,0,1:T(4,128)} %copy.225, s32[5]{0:T(128)S(1)} %copy-done.14, s32[4]{0:T(128)S(1)} %get-tuple-element.7), kind=kOutput, calls=%fused_computation.31 | convolution fusion | flops 15728660 | bytes 2359332 | tf_op jit(solution)/shard_map/ws,spc->wpc/dot_general | solution.py:143
  67.8 1.4 %convolution_bitcast_fusion.1 = f32[5,1,256,256]{3,0,2,1:T(8,128)S(1)} fusion(f32[4,256,256]{2,0,1:T(4,128)S(1)} %copy-done.3, s32[5]{0:T(128)S(1)} %copy-done.14, s32[4]{0:T(128)S(1)} %get-tuple-element.7), kind=kOutput, calls=%fused_computation.32 | convolution fusion | flops 15728660 | bytes 2359332 | tf_op jit(solution)/shard_map/ws,spc->wpc/dot_general | solution.py:137
  70.5 1.5 %fusion.62 = (bf16[1,2,256,256]{3,0,2,1:T(2,128)(2,1)S(1)}, bf16[1,2,256,256]{3,0,2,1:T(2,128)(2,1)S(1)}, bf16[1,2,256,256]{3,0,2,1:T(2,128)(2,1)S(1)}, bf16[1,2,256,256]{3,0,2,1:T(2,128)(2,1)S(1)}) fusion(bf16[5,2,256,256]{3,0,2,1:T(8,128)(2,1)S(1)} %fusion), kind=kLoop, calls=%fused_computation.102 | loop fusion | bytes 2097152 | tf_op jit(solution)/shard_map/slice | solution.py:154
  74.3 2.0 %collective-permute-start.5 = (bf16[2,256,256]{2,1,0:T(8,128)(2,1)}, bf16[2,256,256]{2,1,0:T(8,128)(2,1)}, u32[]{:S(2)}, u32[]{:S(2)}) collective-permute-start(bf16[2,256,256]{2,1,0:T(8,128)(2,1)} %bitcast.192), channel_id=1, source_target_pairs={{0,252},{4,0},{8,4},{12,8},{16,12},{20,16},{24,20},{28,24},{32,28}... | collective-permute-start | bytes 786440 | tf_op jit(solution)/shard_map/ppermute | solution.py:15
  76.4 4.8 %collective-permute-start.4 = (bf16[2,256,256]{2,1,0:T(8,128)(2,1)S(1)}, bf16[2,256,256]{2,1,0:T(8,128)(2,1)}, u32[]{:S(2)}, u32[]{:S(2)}) collective-permute-start(bf16[2,256,256]{2,1,0:T(8,128)(2,1)S(1)} %bitcast.219), channel_id=1, source_target_pairs={{0,248},{4,252},{8,0},{12,4},{16,8},{20,12},{24,16},{28,20},{32,24... | collective-permute-start | bytes 786440 | tf_op jit(solution)/shard_map/ppermute | solution.py:15
  81.2 1.6 %fusion.9 = bf16[4,64,2,8,128]{4,1,3,2,0:T(8,128)(2,1)} fusion(f32[4,2,128,8,64]{2,4,3,1,0:T(8,128)S(1)} %copy-done.2, bf16[4,2,8,64,64]{3,4,2,1,0:T(8,128)(2,1)S(1)} %copy-done.8, bf16[4,64,2,128,1]{3,2,1,0,4:T(2,128)(2,1)S(1)} %bitcast.204), kind=kOutput, calls=%fused_computation.17 | convolution fusion | flops 68681728 | bytes 3801088 | tf_op jit(solution)/shard_map/nkgtj,njkd->ntkgd/dot_general | solution.py:119
  86.0 1.9 %copy.219 = bf16[4,64,2,8,128]{4,3,2,1,0:T(8,128)(2,1)S(1)} copy(bf16[4,64,2,8,128]{4,1,3,2,0:T(8,128)(2,1)} %fusion.9) | data formatting | bytes 2097152 | tf_op jit(solution)/shard_map/convert_element_type | solution.py:122
  90.2 2.3 %fusion.36 = f32[1,2,256,256]{3,0,2,1:T(1,128)S(1)} fusion(f32[5,1,256,256]{3,0,2,1:T(8,128)} %copy-done.1, f32[5,1,256,256]{3,0,2,1:T(8,128)S(1)} %convolution_bitcast_fusion), kind=kLoop, calls=%fused_computation.56 | loop fusion | flops 131072 | bytes 3145728 | tf_op jit(solution)/shard_map/stack | solution.py:149
  92.5 1.3 %fusion.40 = bf16[2,256,256]{2,1,0:T(8,128)(2,1)S(1)} fusion(f32[1,2,256,256]{3,0,2,1:T(1,128)S(1)} %fusion.36, bf16[2,256,256]{2,1,0:T(8,128)(2,1)} %collective-permute-done.7, bf16[2,256,256]{2,1,0:T(8,128)(2,1)} %collective-permute-done.6, bf16[2,256,256]{2,1,0:T(8,128)(2,1)} %collective-permute-done.5, bf16[2,256,256]{2,1,0:T(8,128)(2,1)} %collective-permute-done.4), kind=kLoop, calls=%fused_computation.61 | loop fusion | flops 1179648 | bytes 1835008 | tf_op jit(solution)/shard_map/convert_element_type | solution.py:21
  94.8 3.4 %all-to-all-start.1 = ((bf16[2,256,256]{2,0,1:T(2,128)(2,1)}), bf16[2,256,256]{2,0,1:T(2,128)(2,1)S(1)}, u32[]{:S(2)}, u32[]{:S(2)}) async-start(bf16[2,256,256]{2,0,1:T(2,128)(2,1)} %copy.226), calls=%async_computation.1 | async-start | bytes 524288 | tf_op jit(solution)/shard_map/all_to_all | solution.py:156
  99.0 4.8 %all-to-all-done.1 = bf16[2,256,256]{2,0,1:T(2,128)(2,1)S(1)} async-done(((bf16[2,256,256]{2,0,1:T(2,128)(2,1)}), bf16[2,256,256]{2,0,1:T(2,128)(2,1)S(1)}, u32[]{:S(2)}, u32[]{:S(2)}) %all-to-all-start.1) | async-done | bytes 262176 | tf_op jit(solution)/shard_map/all_to_all | solution.py:156
  (95 shorter events, 29.4 us)
Async XLA Ops:
  0.6 8.7 %copy-start = (s32[64]{0:T(128)S(1)}, s32[64]{0:T(128)}, u32[]{:S(2)}) copy-start(s32[64]{0:T(128)} %param.15) | copy-start | bytes 772
  0.6 7.5 %copy-start.17 = (s32[4]{0:T(128)S(1)}, s32[4]{0:T(128)}, u32[]{:S(2)}) copy-start(s32[4]{0:T(128)} %param.17) | copy-start | bytes 52
  0.7 9.8 %copy-start.10 = (bf16[256,256]{1,0:T(8,128)(2,1)S(1)}, bf16[256,256]{1,0:T(8,128)(2,1)}, u32[]{:S(2)}) copy-start(bf16[256,256]{1,0:T(8,128)(2,1)} %param.10) | copy-start | bytes 393220
  0.7 9.8 %copy-start.4 = (bf16[256,2048]{1,0:T(8,128)(2,1)S(1)}, bf16[256,2048]{1,0:T(8,128)(2,1)}, u32[]{:S(2)}) copy-start(bf16[256,2048]{1,0:T(8,128)(2,1)} %param.9) | copy-start | bytes 3145732
  3.3 10.4 %all-to-all-start = ((bf16[4,2,16384]{2,1,0:T(2,128)(2,1)}), bf16[4,2,16384]{2,1,0:T(2,128)(2,1)S(1)}, u32[]{:S(2)}, u32[]{:S(2)}) async-start(bf16[4,2,16384]{2,1,0:T(2,128)(2,1)} %reshape.188), calls=%async_computation | async-start | bytes 524288 | tf_op jit(solution)/shard_map/all_to_all | solution.py:45
  10.7 1.8 %copy-start.18 = (s32[4]{0:T(128)S(1)}, s32[4]{0:T(128)}, u32[]{:S(2)}) copy-start(s32[4]{0:T(128)} %and_select_fusion) | copy-start | bytes 52
  17.0 17.1 %collective-permute-start.3 = (bf16[2,256,256]{2,1,0:T(8,128)(2,1)}, bf16[2,256,256]{2,1,0:T(8,128)(2,1)}, u32[]{:S(2)}, u32[]{:S(2)}) collective-permute-start(bf16[2,256,256]{2,1,0:T(8,128)(2,1)} %bitcast.4), channel_id=1, source_target_pairs={{0,8},{4,12},{8,16},{12,20},{16,24},{20,28},{24,32},{28,36},{32,40... | collective-permute-start | bytes 786440 | tf_op jit(solution)/shard_map/ppermute | solution.py:15
  18.3 17.6 %collective-permute-start.2 = (bf16[2,256,256]{2,1,0:T(8,128)(2,1)}, bf16[2,256,256]{2,1,0:T(8,128)(2,1)}, u32[]{:S(2)}, u32[]{:S(2)}) collective-permute-start(bf16[2,256,256]{2,1,0:T(8,128)(2,1)} %bitcast.4), channel_id=1, source_target_pairs={{0,4},{4,8},{8,12},{12,16},{16,20},{20,24},{24,28},{28,32},{32,36}... | collective-permute-start | bytes 786440 | tf_op jit(solution)/shard_map/ppermute | solution.py:15
  21.9 15.8 %collective-permute-start.1 = (bf16[2,256,256]{2,1,0:T(8,128)(2,1)}, bf16[2,256,256]{2,1,0:T(8,128)(2,1)}, u32[]{:S(2)}, u32[]{:S(2)}) collective-permute-start(bf16[2,256,256]{2,1,0:T(8,128)(2,1)} %bitcast.4), channel_id=1, source_target_pairs={{0,252},{4,0},{8,4},{12,8},{16,12},{20,16},{24,20},{28,24},{32,28}... | collective-permute-start | bytes 786440 | tf_op jit(solution)/shard_map/ppermute | solution.py:15
  21.9 17.6 %collective-permute-start = (bf16[2,256,256]{2,1,0:T(8,128)(2,1)}, bf16[2,256,256]{2,1,0:T(8,128)(2,1)}, u32[]{:S(2)}, u32[]{:S(2)}) collective-permute-start(bf16[2,256,256]{2,1,0:T(8,128)(2,1)} %bitcast.4), channel_id=1, source_target_pairs={{0,248},{4,252},{8,0},{12,4},{16,8},{20,12},{24,16},{28,20},{32,24... | collective-permute-start | bytes 786440 | tf_op jit(solution)/shard_map/ppermute | solution.py:15
  41.3 1.6 %copy-start.13 = (pred[4,256]{1,0:T(4,128)(4,1)S(1)}, pred[4,256]{1,0:T(4,128)(4,1)}, u32[]{:S(2)}) copy-start(pred[4,256]{1,0:T(4,128)(4,1)} %iota_compare_fusion.1) | copy-start | bytes 3076
  42.9 0.8 copy-start.9
  44.4 1.7 %copy-start.5 = (bf16[32,8,16,128]{3,2,1,0:T(8,128)(2,1)S(1)}, bf16[32,8,16,128]{3,2,1,0:T(8,128)(2,1)}, u32[]{:S(2)}) copy-start(bf16[32,8,16,128]{3,2,1,0:T(8,128)(2,1)} %copy.274) | copy-start | bytes 3145732
  44.4 1.7 %copy-start.16 = (bf16[4,64]{1,0:T(4,128)(2,1)S(1)}, bf16[4,64]{1,0:T(4,128)(2,1)}, u32[]{:S(2)}) copy-start(bf16[4,64]{1,0:T(4,128)(2,1)} %get-tuple-element.16) | copy-start | bytes 1540
  51.1 1.9 %copy-start.12 = (bf16[4,64,2,128]{3,2,1,0:T(2,128)(2,1)S(1)}, bf16[4,64,2,128]{3,2,1,0:T(2,128)(2,1)}, u32[]{:S(2)}) copy-start(bf16[4,64,2,128]{3,2,1,0:T(2,128)(2,1)} %reshape.156) | copy-start | bytes 393220
  51.1 1.9 %copy-start.15 = (f32[4,64]{1,0:T(4,128)S(1)}, f32[4,64]{1,0:T(4,128)}, u32[]{:S(2)}) copy-start(f32[4,64]{1,0:T(4,128)} %get-tuple-element.17) | copy-start | bytes 3076
  60.4 2.0 %copy-start.7 = (f32[4,2,128,256,1]{3,2,4,1,0:T(8,128)S(1)}, f32[4,2,128,256,1]{3,2,4,1,0:T(8,128)}, u32[]{:S(2)}) copy-start(f32[4,2,128,256,1]{3,2,4,1,0:T(8,128)} %fusion.26) | copy-start | bytes 3145732
  62.4 2.6 %copy-start.14 = (s32[5]{0:T(128)S(1)}, s32[5]{0:T(128)}, u32[]{:S(2)}) copy-start(s32[5]{0:T(128)} %iota_add_fusion) | copy-start | bytes 64
  65.1 2.7 %copy-start.3 = (f32[4,256,256]{2,0,1:T(4,128)S(1)}, f32[4,256,256]{2,0,1:T(4,128)}, u32[]{:S(2)}) copy-start(f32[4,256,256]{2,0,1:T(4,128)} %copy.224) | copy-start | bytes 3145732
  69.2 1.3 %copy-start.1 = (f32[5,1,256,256]{3,0,2,1:T(8,128)}, f32[5,1,256,256]{3,0,2,1:T(8,128)S(1)}, u32[]{:S(2)}) copy-start(f32[5,1,256,256]{3,0,2,1:T(8,128)S(1)} %convolution_bitcast_fusion.1) | copy-start | bytes 3932164
  72.0 9.1 %copy-start.2 = (f32[4,2,128,8,64]{2,4,3,1,0:T(8,128)S(1)}, f32[4,2,128,8,64]{2,4,3,1,0:T(8,128)}, u32[]{:S(2)}) copy-start(f32[4,2,128,8,64]{2,4,3,1,0:T(8,128)} %fusion.65) | copy-start | bytes 6291460
  72.0 9.1 %copy-start.8 = (bf16[4,2,8,64,64]{3,4,2,1,0:T(8,128)(2,1)S(1)}, bf16[4,2,8,64,64]{3,4,2,1,0:T(8,128)(2,1)}, u32[]{:S(2)}) copy-start(bf16[4,2,8,64,64]{3,4,2,1,0:T(8,128)(2,1)} %fusion.11) | copy-start | bytes 1572868
  74.3 18.2 %collective-permute-start.5 = (bf16[2,256,256]{2,1,0:T(8,128)(2,1)}, bf16[2,256,256]{2,1,0:T(8,128)(2,1)}, u32[]{:S(2)}, u32[]{:S(2)}) collective-permute-start(bf16[2,256,256]{2,1,0:T(8,128)(2,1)} %bitcast.192), channel_id=1, source_target_pairs={{0,252},{4,0},{8,4},{12,8},{16,12},{20,16},{24,20},{28,24},{32,28}... | collective-permute-start | bytes 786440 | tf_op jit(solution)/shard_map/ppermute | solution.py:15
  76.3 16.1 %collective-permute-start.6 = (bf16[2,256,256]{2,1,0:T(8,128)(2,1)}, bf16[2,256,256]{2,1,0:T(8,128)(2,1)}, u32[]{:S(2)}, u32[]{:S(2)}) collective-permute-start(bf16[2,256,256]{2,1,0:T(8,128)(2,1)} %bitcast.191), channel_id=1, source_target_pairs={{0,4},{4,8},{8,12},{12,16},{16,20},{20,24},{24,28},{28,32},{32,36}... | collective-permute-start | bytes 786440 | tf_op jit(solution)/shard_map/ppermute | solution.py:15
  76.4 16.2 %collective-permute-start.7 = (bf16[2,256,256]{2,1,0:T(8,128)(2,1)}, bf16[2,256,256]{2,1,0:T(8,128)(2,1)}, u32[]{:S(2)}, u32[]{:S(2)}) collective-permute-start(bf16[2,256,256]{2,1,0:T(8,128)(2,1)} %bitcast.190), channel_id=1, source_target_pairs={{0,8},{4,12},{8,16},{12,20},{16,24},{20,28},{24,32},{28,36},{32,40... | collective-permute-start | bytes 786440 | tf_op jit(solution)/shard_map/ppermute | solution.py:15
  76.4 16.2 %collective-permute-start.4 = (bf16[2,256,256]{2,1,0:T(8,128)(2,1)S(1)}, bf16[2,256,256]{2,1,0:T(8,128)(2,1)}, u32[]{:S(2)}, u32[]{:S(2)}) collective-permute-start(bf16[2,256,256]{2,1,0:T(8,128)(2,1)S(1)} %bitcast.219), channel_id=1, source_target_pairs={{0,248},{4,252},{8,0},{12,4},{16,8},{20,12},{24,16},{28,20},{32,24... | collective-permute-start | bytes 786440 | tf_op jit(solution)/shard_map/ppermute | solution.py:15
  82.7 1.2 %copy-start.11 = (bf16[4,64,2,128]{3,1,2,0:T(8,128)(2,1)S(1)}, bf16[4,64,2,128]{3,1,2,0:T(8,128)(2,1)}, u32[]{:S(2)}) copy-start(bf16[4,64,2,128]{3,1,2,0:T(8,128)(2,1)} %fusion.25) | copy-start | bytes 393220
  82.7 1.3 %copy-start.6 = (bf16[4,64,2,8,128]{4,1,3,2,0:T(8,128)(2,1)S(1)}, bf16[4,64,2,8,128]{4,1,3,2,0:T(8,128)(2,1)}, u32[]{:S(2)}) copy-start(bf16[4,64,2,8,128]{4,1,3,2,0:T(8,128)(2,1)} %get-tuple-element.26) | copy-start | bytes 3145732
  94.8 8.9 %all-to-all-start.1 = ((bf16[2,256,256]{2,0,1:T(2,128)(2,1)}), bf16[2,256,256]{2,0,1:T(2,128)(2,1)S(1)}, u32[]{:S(2)}, u32[]{:S(2)}) async-start(bf16[2,256,256]{2,0,1:T(2,128)(2,1)} %copy.226), calls=%async_computation.1 | async-start | bytes 524288 | tf_op jit(solution)/shard_map/all_to_all | solution.py:156
where the time goes:
time: 107 us; the launch traced here: 106 us
  local copies, waits for them, and re-layouts  35.9 us (34%)
  matrix products  25.6 us (24%)
  starting transfers between devices  25.2 us (24%)
  other arithmetic  13.3 us (12%)
  waiting for transfers between devices  5.29 us (5%)
  between operations  1.08 us (1%)
    ppermute x8, starting transfers between devices, passed_along(): return lax.ppermute(x, axis, [(i, (i + by) % size) for i in range(size)])  17 us
    unnamed x46, local copies, waits for them, and re-layouts  8.13 us
    ppermute x4, local copies, waits for them, and re-layouts, passed_along(): return lax.ppermute(x, axis, [(i, (i + by) % size) for i in range(size)])  7.15 us
    all_to_all x1, starting transfers between devices, on_device(): lax.all_to_all(stacked, 'head', split_axis=2, concat_axis=1, tiled=True)  4.84 us
    all_to_all x1, waiting for transfers between devices, on_device(): lax.all_to_all(for_sending(summed), 'head', split_axis=1, concat_axis=2,...  4.78 us
    all_to_all x1, starting transfers between devices, on_device(): lax.all_to_all(for_sending(summed), 'head', split_axis=1, concat_axis=2,...  3.41 us
    dot_general x1, matrix products, on_device(): jnp.einsum('nkgtj,ntkgd->njkd', head_weights, grad_live, preferred_elemen...  3.34 us
    all_to_all x3, local copies, waits for them, and re-layouts, on_device(): lax.all_to_all(stacked, 'head', split_axis=2, concat_axis=1, tiled=True)  3.28 us
  transfers between devices with their start and end apart: 10, of which 2 were waited for; matrix products, arithmetic and copies ran while one was open for 28% of the time, Pallas kernels for 0%

commit v1 on v0

v1 whole, which is shorter than its diff:
```python
import functools
import math

import jax
import jax.numpy as jnp
from jax import lax
from jax.experimental import pallas as pl
from jax.experimental.pallas import tpu as pltpu
from jax.sharding import PartitionSpec as P

HEAD_SIZE = 128
PLEN = 256
MAX_SPREAD = 2
REACH = 2 * MAX_SPREAD + 1
MESH = pl.DeviceIdType.MESH
SCALING = 1.0 / math.sqrt(HEAD_SIZE)
F32 = jnp.float32
BF16 = jnp.bfloat16


def dot(a, b, dims):
    return lax.dot_general(a, b, (dims, ((), ())), preferred_element_type=F32)


NN = ((1,), (0,))
NT = ((1,), (1,))
TN = ((0,), (0,))


def kernel(sizes, *refs):
    devices, heads, slots, rows, kvh, group = sizes
    (plen_hbm, rlen_hbm, rprompt_hbm, q_hbm, do_hbm, ak_hbm, av_hbm, pk_hbm, pv_hbm,
     o_v, dq_v, gak_v, gav_v, gpk_out, gpv_out,
     plen_ref, rlen_ref, rprompt_ref,
     q_v, do_v, ak_v, av_v, qt_v, dot_v, p_v, w_v, ds_v) = refs[:27]
    pairs = [(hd, w) for hd in range(kvh) for w in range(2)]
    per_pair = refs[27:27 + 8 * len(pairs)]
    (kv, part, sib_out, sib_in, y_out, y_in, own, x_out) = [
        dict(zip(pairs, per_pair[i * len(pairs):(i + 1) * len(pairs)])) for i in range(8)
    ]
    (in_sem, x_send, x_recv, x_own, y_send, y_recv, s_send, s_recv,
     bs_send, bs_recv, by_send, by_recv, bx_send, bx_recv, bx_own) = refs[27 + 8 * len(pairs):]

    me = lax.axis_index("dp")
    h = lax.axis_index("head")
    core = lax.rem(me, 2)
    sibling = me + 1 - 2 * core
    up = lax.rem(me + 2, devices)
    down = lax.rem(me + devices - 2, devices)
    span = PLEN // heads
    width = kvh * HEAD_SIZE
    lanes = group * rows
    chunk = min(256, lanes)
    per = chunk // rows
    all_rows = PLEN + rows

    own_in = {}
    for hd, w in pairs:
        src = (pk_hbm, pv_hbm)[w]
        cols = pl.ds(pl.multiple_of(h * width + hd * HEAD_SIZE, HEAD_SIZE), HEAD_SIZE)
        mine = pl.ds(pl.multiple_of(h * span, span), span)
        own_in[hd, w] = pltpu.make_async_copy(
            src.at[:, cols], kv[hd, w].at[MAX_SPREAD, mine], x_own.at[hd, w])
        own_in[hd, w].start()
    loads = [
        pltpu.make_async_copy(src, dst, in_sem.at[i])
        for i, (src, dst) in enumerate(
            [(q_hbm, q_v), (do_hbm, do_v), (ak_hbm, ak_v), (av_hbm, av_v),
             (plen_hbm, plen_ref), (rlen_hbm, rlen_ref), (rprompt_hbm, rprompt_ref)])
    ]
    for load in loads:
        load.start()

    def remote(src, dst, send, recv, **where):
        return pltpu.make_async_remote_copy(
            src_ref=src, dst_ref=dst, send_sem=send, recv_sem=recv,
            device_id=where, device_id_type=MESH)

    peers = [lax.rem(h + p, heads) for p in range(1, heads)]
    order = [p for p in range(1, heads) if p != heads // 2] + [heads // 2]

    barrier = pltpu.get_barrier_semaphore()
    for p in peers:
        pl.semaphore_signal(barrier, inc=1, device_id={"head": p}, device_id_type=MESH)
    for d in (sibling, up, down):
        pl.semaphore_signal(barrier, inc=1, device_id={"dp": d}, device_id_type=MESH)
    pl.semaphore_wait(barrier, len(peers) + 3)

    x_in = {}
    for hd, w in pairs:
        src = (pk_hbm, pv_hbm)[w]
        for p in order:
            to = peers[p - 1]
            cols = pl.ds(pl.multiple_of(to * width + hd * HEAD_SIZE, HEAD_SIZE), HEAD_SIZE)
            x_in[hd, w, p] = remote(
                src.at[:, cols], kv[hd, w].at[MAX_SPREAD, mine],
                x_send.at[hd, w, p - 1], x_recv.at[hd, w, p - 1], head=to)
            x_in[hd, w, p].start()

    y_copies, s_copies, r_copies = {}, {}, {}

    def forward(hd, w, piece, span_rows):
        ref = kv[hd, w]
        src = ref.at[MAX_SPREAD, span_rows]
        y_copies[hd, w, piece] = [
            remote(src, ref.at[0, span_rows], y_send.at[hd, w, piece, 0],
                   y_recv.at[hd, w, piece, 0], dp=up),
            remote(src, ref.at[4, span_rows], y_send.at[hd, w, piece, 1],
                   y_recv.at[hd, w, piece, 1], dp=down),
        ]
        s_copies[hd, w, piece] = remote(
            src, ref.at[1 + 2 * core, span_rows], s_send.at[hd, w, piece, 0],
            s_recv.at[hd, w, piece, 0], dp=sibling)
        r_copies[hd, w, piece] = remote(
            ref.at[4 - 4 * core, span_rows], ref.at[3 - 2 * core, span_rows],
            s_send.at[hd, w, piece, 1], s_recv.at[hd, w, piece, 1], dp=sibling)
        for c in y_copies[hd, w, piece]:
            c.start()
        s_copies[hd, w, piece].start()

    pieces = {pair: [0] for pair in pairs}
    pieces[0, 0] = [0] + order

    def forward_all(hd, w):
        if len(pieces[hd, w]) > 1:
            for p in pieces[hd, w]:
                if p == 0:
                    own_in[hd, w].wait()
                else:
                    x_in[hd, w, p].wait_recv()
                source = lax.rem(h + heads - p, heads)
                forward(hd, w, p, pl.ds(pl.multiple_of(source * span, span), span))
        else:
            own_in[hd, w].wait()
            for p in order:
                x_in[hd, w, p].wait_recv()
            forward(hd, w, 0, pl.ds(0, PLEN))

    def relay_in(hd, w):
        for p in pieces[hd, w]:
            for c in y_copies[hd, w, p]:
                c.wait_recv()
            r_copies[hd, w, p].start()

    def arrived(hd, w):
        for p in pieces[hd, w]:
            s_copies[hd, w, p].wait_recv()
            r_copies[hd, w, p].wait_recv()

    def rows_of(s):
        return pl.ds(pl.multiple_of(s * rows, rows), rows)

    def columns(hd, c):
        first = hd * group + c * per
        return [slice((first + g) * HEAD_SIZE, (first + g + 1) * HEAD_SIZE) for g in range(per)]

    def stacked(ref, hd, s, c):
        return jnp.concatenate([ref[rows_of(s), col] for col in columns(hd, c)], axis=0)

    def relative(s):
        return lax.rem(rprompt_ref[s] - me + (devices + MAX_SPREAD), devices)

    def both(hd, w, s):
        rel = jnp.minimum(relative(s), REACH - 1)
        tail = (ak_v, av_v)[w][rows_of(s), hd * HEAD_SIZE:(hd + 1) * HEAD_SIZE]
        return jnp.concatenate([kv[hd, w][rel], tail], axis=0)

    def lanes_of(c):
        return slice(c * chunk, (c + 1) * chunk)

    def prepare(hd, s):
        for c in range(lanes // chunk):
            qt_v[hd, s, :, lanes_of(c)] = stacked(q_v, hd, s, c).T
            dot_v[hd, s, :, lanes_of(c)] = stacked(do_v, hd, s, c).T

    def probabilities(hd, s):
        psize = plen_ref[rprompt_ref[s]]
        rlen = rlen_ref[s]
        keys = both(hd, 0, s)
        live = (lax.rem(lax.broadcasted_iota(jnp.int32, (1, chunk), 1), rows) < rlen).astype(F32)
        head_seen = lax.broadcasted_iota(jnp.int32, (PLEN, chunk), 0) < psize
        tail_seen = lax.broadcasted_iota(jnp.int32, (rows, chunk), 0) <= lax.rem(
            lax.broadcasted_iota(jnp.int32, (rows, chunk), 1), rows)
        dv = jnp.zeros((all_rows, HEAD_SIZE), F32)
        for c in range(lanes // chunk):
            scores = dot(keys, qt_v[hd, s, :, lanes_of(c)], NN)
            masked = jnp.concatenate([
                jnp.where(head_seen, scores[:PLEN], -jnp.inf),
                jnp.where(tail_seen, scores[PLEN:], -jnp.inf)], axis=0)
            top = jnp.max(masked, axis=0, keepdims=True)
            e = jnp.exp2((masked - top) * (SCALING * math.log2(math.e)))
            prob = e * (live / jnp.sum(e, axis=0, keepdims=True))
            p_v[s, :, lanes_of(c)] = prob
            weights = prob.astype(BF16)
            w_v[hd, s, :, lanes_of(c)] = weights
            dv += dot(weights, stacked(do_v, hd, s, c), NN)
        part[hd, 1][s] = dv[:PLEN]
        gav_v[rows_of(s), hd * HEAD_SIZE:(hd + 1) * HEAD_SIZE] = dv[PLEN:].astype(BF16)

    def gradients(hd, s):
        values = both(hd, 1, s)
        dk = jnp.zeros((all_rows, HEAD_SIZE), F32)
        for c in range(lanes // chunk):
            prob = p_v[s, :, lanes_of(c)]
            gprob = dot(values, dot_v[hd, s, :, lanes_of(c)], NN)
            delta = jnp.sum(prob * gprob, axis=0, keepdims=True)
            gscores = (prob * (gprob - delta)).astype(BF16)
            ds_v[hd, s, :, lanes_of(c)] = gscores
            dk += dot(gscores, stacked(q_v, hd, s, c), NN)
        dk = dk * SCALING
        part[hd, 0][s] = dk[:PLEN]
        gak_v[rows_of(s), hd * HEAD_SIZE:(hd + 1) * HEAD_SIZE] = dk[PLEN:].astype(BF16)

    def row_outputs(hd, s):
        keys_t = both(hd, 0, s).T
        values_t = both(hd, 1, s).T
        for c in range(lanes // chunk):
            out = dot(values_t, w_v[hd, s, :, lanes_of(c)], NN).astype(BF16).T
            dq = (dot(keys_t, ds_v[hd, s, :, lanes_of(c)], NN) * SCALING).astype(BF16).T
            for g, col in enumerate(columns(hd, c)):
                o_v[rows_of(s), col] = out[g * rows:(g + 1) * rows]
                dq_v[rows_of(s), col] = dq[g * rows:(g + 1) * rows]

    def summed(pair, offset):
        total = None
        for s in range(slots):
            pick = jnp.where(relative(s) == offset, 1.0, 0.0).astype(F32)
            term = part[pair][s] * pick
            total = term if total is None else total + term
        return total

    direct, relayed = 4 * core, 4 - 4 * core
    direct_to = lax.rem(me + devices - 2 + 4 * core, devices)
    relay_to = lax.rem(me + devices + 2 - 4 * core, devices)
    b_sib, b_direct, b_relay, b_x, b_own = {}, {}, {}, {}, {}
    for pair in pairs:
        hd, w = pair
        b_sib[pair] = [
            remote(sib_out[pair].at[i], sib_in[pair].at[i], bs_send.at[hd, w, i],
                   bs_recv.at[hd, w, i], dp=sibling) for i in range(2)
        ]
        b_direct[pair] = remote(y_out[pair].at[0], y_in[pair].at[core], by_send.at[hd, w, 0],
                                by_recv.at[hd, w, core], dp=direct_to)
        b_relay[pair] = remote(y_out[pair].at[1], y_in[pair].at[1 - core],
                               by_send.at[hd, w, 1], by_recv.at[hd, w, 1 - core], dp=relay_to)
        dst = (gpk_out, gpv_out)[w]
        cols = pl.ds(pl.multiple_of(h * width + hd * HEAD_SIZE, HEAD_SIZE), HEAD_SIZE)
        b_x[pair] = []
        for p in order:
            to = peers[p - 1]
            theirs = pl.ds(pl.multiple_of(to * span, span), span)
            b_x[pair].append(remote(
                x_out[pair].at[theirs], dst.at[:, cols],
                bx_send.at[hd, w, p - 1], bx_recv.at[hd, w, p - 1], head=to))
        b_own[pair] = pltpu.make_async_copy(
            x_out[pair].at[mine], dst.at[:, cols], bx_own.at[hd, w])

    def back_first(pair):
        for i in range(2):
            sib_out[pair][i] = summed(pair, 1 + 2 * i).astype(BF16)
            b_sib[pair][i].start()
        y_out[pair][0] = summed(pair, direct).astype(BF16)
        b_direct[pair].start()

    def back_relay(pair):
        carry = summed(pair, relayed)
        own[pair][...] = summed(pair, MAX_SPREAD)
        for c in b_sib[pair]:
            c.wait_recv()
        y_out[pair][1] = (carry + sib_in[pair][1 - core].astype(F32)).astype(BF16)
        b_relay[pair].start()
        own[pair][...] += sib_in[pair][core].astype(F32)

    def back_last(pair):
        b_direct[pair].wait_recv()
        b_relay[pair].wait_recv()
        x_out[pair][...] = (own[pair][...] + y_in[pair][0].astype(F32)
                            + y_in[pair][1].astype(F32)).astype(BF16)
        for c in b_x[pair]:
            c.start()
        b_own[pair].start()

    def each_slot(work, hd, at=()):
        def step(s, carry):
            for when, what, *args in at:
                pl.when(s == when)(functools.partial(what, *args))
            work(hd, s)
            return carry

        lax.fori_loop(0, slots, step, 0)

    last = slots - 1
    forward_all(0, 0)
    forward_all(0, 1)
    for load in loads:
        load.wait()
    each_slot(prepare, 0)
    for hd, w in pairs[2:]:
        forward_all(hd, w)
    relay_in(0, 0)
    for hd in range(1, kvh):
        each_slot(prepare, hd)
    arrived(0, 0)

    back_steps = []

    for hd in range(kvh):
        at = []
        if hd == 0:
            at.append((1, relay_in, 0, 1))
        else:
            at.append((0, back_last, (hd - 1, 1)))
            at.append((1, back_relay, (hd - 1, 0)))
        if hd + 1 < kvh:
            at.append((last, relay_in, hd + 1, 0))
        each_slot(probabilities, hd, at)
        back_first((hd, 1))
        arrived(hd, 1)
        at = [(1, back_relay, (hd, 1))]
        if hd > 0:
            at.append((0, back_last, (hd - 1, 0)))
        if hd + 1 < kvh:
            at.append((last, relay_in, hd + 1, 1))
        each_slot(gradients, hd, at)
        back_first((hd, 0))
        if hd + 1 < kvh:
            arrived(hd + 1, 0)

    end = kvh - 1
    for hd in range(kvh):
        at = []
        if hd == 0:
            at = [(1, back_last, (end, 1)), (min(2, last), back_relay, (end, 0))]
        if hd == end:
            at.append((min(2, last), back_last, (end, 0)))
        each_slot(row_outputs, hd, at)

    for pair in pairs:
        hd, w = pair
        for p in order:
            x_in[hd, w, p].wait_send()
        for p in pieces[pair]:
            for c in y_copies[hd, w, p] + [s_copies[hd, w, p], r_copies[hd, w, p]]:
                c.wait_send()
        for c in b_sib[pair] + [b_direct[pair], b_relay[pair]]:
            c.wait_send()
        for c in b_x[pair]:
            c.wait()
        b_own[pair].wait()


def finish(o, dq, gak, gav, gpk, gpv, o_out, dq_out, gak_out, gav_out, gpk_out, gpv_out,
           wide_k, wide_v, sem):
    copies = [
        pltpu.make_async_copy(src, dst, sem.at[i])
        for i, (src, dst) in enumerate(
            [(o, o_out), (dq, dq_out), (gak, gak_out), (gav, gav_out),
             (wide_k, gpk_out.at[0]), (wide_v, gpv_out.at[0])])
    ]
    for copy in copies[:4]:
        copy.start()
    wide_k[...] = gpk[...].astype(F32)
    copies[4].start()
    wide_v[...] = gpv[...].astype(F32)
    copies[5].start()
    for copy in copies:
        copy.wait()


def on_device(queries, answer_keys, answer_values, prompt_keys, prompt_values,
              output_gradient, prompt_len, response_len, response_prompt):
    devices, heads = lax.axis_size("dp"), lax.axis_size("head")
    slots = response_len.shape[0]
    token_rows, q_width = queries.shape
    rows = token_rows // slots
    width = answer_keys.shape[1]
    kvh = width // HEAD_SIZE
    group = q_width // width
    lanes = group * rows
    span, full = prompt_keys.shape[1:]
    dma = pltpu.SemaphoreType.DMA
    anywhere = pl.BlockSpec(memory_space=pl.ANY)
    hbm = pl.BlockSpec(memory_space=pltpu.HBM)
    vmem = pl.BlockSpec(memory_space=pltpu.VMEM)
    vm, sm = pltpu.VMEM, pltpu.SMEM
    block = (PLEN, HEAD_SIZE)
    wide = vm((token_rows, q_width), BF16)
    narrow = vm((token_rows, width), BF16)
    turned = vm((kvh, slots, HEAD_SIZE, lanes), BF16)
    square = (PLEN + rows, lanes)
    per_pair = [
        vm((REACH,) + block, BF16), vm((slots,) + block, F32),
        vm((2,) + block, BF16), vm((2,) + block, BF16),
        vm((2,) + block, BF16), vm((2,) + block, BF16),
        vm(block, F32), vm(block, BF16),
    ]
    scratch = [
        sm(prompt_len.shape, jnp.int32), sm(response_len.shape, jnp.int32),
        sm(response_prompt.shape, jnp.int32),
        wide, wide, narrow, narrow, turned, turned, vm((slots,) + square, F32),
        vm((kvh, slots) + square, BF16), vm((kvh, slots) + square, BF16),
    ]
    for shape in per_pair:
        scratch += [shape] * (kvh * 2)
    scratch += [
        dma((7,)),
        dma((kvh, 2, heads - 1)), dma((kvh, 2, heads - 1)), dma((kvh, 2)),
        dma((kvh, 2, heads, 2)), dma((kvh, 2, heads, 2)),
        dma((kvh, 2, heads, 2)), dma((kvh, 2, heads, 2)),
        dma((kvh, 2, 2)), dma((kvh, 2, 2)), dma((kvh, 2, 2)), dma((kvh, 2, 2)),
        dma((kvh, 2, heads - 1)), dma((kvh, 2, heads - 1)), dma((kvh, 2)),
    ]
    sds = jax.ShapeDtypeStruct
    rows_out = [
        sds((token_rows, q_width), BF16), sds((token_rows, q_width), BF16),
        sds((token_rows, width), BF16), sds((token_rows, width), BF16),
    ]
    results = pl.pallas_call(
        functools.partial(kernel, (devices, heads, slots, rows, kvh, group)),
        out_shape=rows_out + [sds((span, full), BF16), sds((span, full), BF16)],
        in_specs=[hbm] * 9,
        out_specs=[vmem] * 4 + [anywhere] * 2,
        scratch_shapes=scratch,
        compiler_params=pltpu.CompilerParams(
            collective_id=0, has_side_effects=True, vmem_limit_bytes=48 * 1024 * 1024),
    )(prompt_len, response_len, response_prompt, queries, output_gradient,
      answer_keys, answer_values, prompt_keys.reshape(span, full),
      prompt_values.reshape(span, full))
    return pl.pallas_call(
        finish,
        out_shape=rows_out + [sds((1, span, full), F32), sds((1, span, full), F32)],
        in_specs=[anywhere] * 4 + [vmem] * 2,
        out_specs=[anywhere] * 6,
        scratch_shapes=[vm((span, full), F32), vm((span, full), F32), dma((6,))],
    )(*results)


def solution(mesh):
    in_specs = (
        P("dp", "head"),
        P("dp", "head"),
        P("dp", "head"),
        P("dp", "head", None),
        P("dp", "head", None),
        P("dp", "head"),
        P(),
        P("dp"),
        P("dp"),
    )
    out_specs = (
        P("dp", "head"),
        P("dp", "head"),
        P("dp", "head"),
        P("dp", "head"),
        P("dp", "head", None),
        P("dp", "head", None),
    )
    return jax.shard_map(
        on_device, mesh=mesh, in_specs=in_specs, out_specs=out_specs, check_vma=False
    )
```

time: 107 us -> 132 us (1.23)
  Pallas kernels: 0 us -> 118 us
  matrix products: 25.6 us -> 0 us
  starting transfers between devices: 25.2 us -> 0 us
  local copies, waits for them, and re-layouts: 35.9 us -> 11.3 us
  other arithmetic: 13.3 us -> 0 us
  waiting for transfers between devices: 5.29 us -> 0 us
    pallas_call x0 -> x2, Pallas kernels: none -> 118 us  [the longest x1 73.6 us: on_device(): pl.pallas_call(finish, out_shape=rows_out + [sds((1, span, full), F32), s...]
    dot_general x14 -> x0, matrix products: 25.6 us -> none  [the longest x1 3.34 us: on_device(): jnp.einsum('nkgtj,ntkgd->njkd', head_weights, grad_live, preferred_elemen...]
    ppermute x8 -> x0, starting transfers between devices: 17 us -> none  [passed_along(): return lax.ppermute(x, axis, [(i, (i + by) % size) for i in range(size)])]
    all_to_all x2 -> x0, starting transfers between devices: 8.25 us -> none  [the longest x1 4.84 us: on_device(): lax.all_to_all(stacked, 'head', split_axis=2, concat_axis=1, tiled=True)]
    ppermute x4 -> x0, local copies, waits for them, and re-layouts: 7.15 us -> none  [passed_along(): return lax.ppermute(x, axis, [(i, (i + by) % size) for i in range(size)])]
    reshape x6 -> x0, local copies, waits for them, and re-layouts: 6.79 us -> none  [the longest x1 1.59 us: on_device(): tail_values = answer_values.reshape(slots, answer_rows, local_kv, HEAD_SIZE)]
    convert_element_type x6 -> x0, local copies, waits for them, and re-layouts: 5.47 us -> none  [the longest x1 1.9 us: on_device(): grad_query = (query_sum * scaling).astype(jnp.bfloat16)]
    all_to_all x2 -> x0, waiting for transfers between devices: 5.27 us -> none  [the longest x1 4.78 us: on_device(): lax.all_to_all(for_sending(summed), 'head', split_axis=1, concat_axis=2,...]
  transfers between devices with their start and end apart: 10 -> 0, of which waited for: 2 -> 0; matrix products, arithmetic and copies ran while one was open for 28% -> 0% of each run, Pallas kernels for 0% -> 0%
where the time goes in v1:
time: 132 us; the launch traced here: 130 us
  Pallas kernels  118 us (89%)
  local copies, waits for them, and re-layouts  11.3 us (9%)
    pallas_call x1, Pallas kernels, on_device(): pl.pallas_call(finish, out_shape=rows_out + [sds((1, span, full), F32), s...  73.6 us
    pallas_call x1, Pallas kernels, on_device(): pl.pallas_call(functools.partial(kernel, (devices, heads, slots, rows, kv...  44.8 us
    unnamed x30, local copies, waits for them, and re-layouts  11.3 us

profile of v1, /device:TPU:1, one launch (start us, length us, event | category | flops | bytes accessed | tf_op | source)
XLA Modules:
  0.0 130.4 jit_solution(11420244623588442753)
XLA Ops:
  0.6 0.0 copy-start.12
  0.6 0.0 copy-start.13
  0.7 0.0 copy-start.14
  0.7 0.6 copy-done.12
  1.3 0.0 copy-done.13
  1.3 0.0 copy-done.14
  1.3 0.0 copy-start
  1.3 1.2 copy-done
  2.5 0.0 copy-start.1
  2.6 1.2 copy-done.1
  3.8 0.0 copy-start.8
  3.8 0.9 copy-done.8
  4.7 0.0 copy-start.9
  4.7 0.9 copy-done.9
  5.6 0.0 copy-start.10
  5.6 0.9 copy-done.10
  6.5 0.0 copy-start.11
  6.5 0.9 copy-done.11
  7.4 44.8 %shard_map.136 = (bf16[256,2048]{1,0:T(8,128)(2,1)S(1)}, bf16[256,2048]{1,0:T(8,128)(2,1)S(1)}, bf16[256,256]{1,0:T(8,128)(2,1)S(1)}, bf16[256,256]{1,0:T(8,128)...) custom-call(s32[64]{0:T(128)S(1)} %copy-done.12, s32[4]{0:T(128)S(1)} %copy-done.13, ...), custom_call_target="tpu_custom_call" | custom-call | tf_op jit(solution)/shard_map/pallas_call | solution.py:418
  52.2 0.0 copy-start.2
  52.2 1.0 copy-done.2
  53.2 0.0 copy-start.3
  53.2 1.0 copy-done.3
  54.2 0.0 copy-start.4
  54.2 0.6 copy-done.4
  54.8 0.0 copy-start.5
  54.8 0.6 copy-done.5
  55.5 0.0 copy-start.6
  55.5 0.6 copy-done.6
  56.1 0.0 copy-start.7
  56.1 0.7 copy-done.7
  56.8 73.6 %shard_map.137 = (bf16[256,2048]{1,0:T(8,128)(2,1)}, bf16[256,2048]{1,0:T(8,128)(2,1)}, bf16[256,256]{1,0:T(8,128)(2,1)}, bf16[256,256]{1,0:T(8,128)(2,1)}, f32[...) custom-call(bf16[256,2048]{1,0:T(8,128)(2,1)} %copy-done.2, bf16[256,2048]{1,0:T(8,128)(2,1)} %copy-done.3, ...), custom_call_target="tpu_custom_call" | custom-call | tf_op jit(solution)/shard_map/pallas_call | solution.py:429
Async XLA Ops:
  0.6 0.7 copy-start.12
  0.6 0.7 copy-start.13
  0.7 0.7 copy-start.14
  1.3 1.2 copy-start
  2.5 1.2 copy-start.1
  3.8 0.9 copy-start.8
  4.7 0.9 copy-start.9
  5.6 0.9 copy-start.10
  6.5 0.9 copy-start.11
  52.2 1.0 copy-start.2
  53.2 1.0 copy-start.3
  54.2 0.6 copy-start.4
  54.8 0.7 copy-start.5
  55.5 0.6 copy-start.6
  56.1 0.7 copy-start.7

commit v2 on v1

--- a/solution.py
+++ b/solution.py
@@ -32,14 +32,14 @@
     (plen_hbm, rlen_hbm, rprompt_hbm, q_hbm, do_hbm, ak_hbm, av_hbm, pk_hbm, pv_hbm,
      o_v, dq_v, gak_v, gav_v, gpk_out, gpv_out,
      plen_ref, rlen_ref, rprompt_ref,
-     q_v, do_v, ak_v, av_v, qt_v, dot_v, p_v, w_v, ds_v) = refs[:27]
+     q_v, do_v, ak_v, av_v, p_v, w_v, ds_v) = refs[:25]
     pairs = [(hd, w) for hd in range(kvh) for w in range(2)]
-    per_pair = refs[27:27 + 8 * len(pairs)]
+    per_pair = refs[25:25 + 8 * len(pairs)]
     (kv, part, sib_out, sib_in, y_out, y_in, own, x_out) = [
         dict(zip(pairs, per_pair[i * len(pairs):(i + 1) * len(pairs)])) for i in range(8)
     ]
     (in_sem, x_send, x_recv, x_own, y_send, y_recv, s_send, s_recv,
-     bs_send, bs_recv, by_send, by_recv, bx_send, bx_recv, bx_own) = refs[27 + 8 * len(pairs):]
+     bs_send, bs_recv, by_send, by_recv, bx_send, bx_recv, bx_own) = refs[25 + 8 * len(pairs):]
 
     me = lax.axis_index("dp")
     h = lax.axis_index("head")
@@ -168,11 +168,6 @@
     def lanes_of(c):
         return slice(c * chunk, (c + 1) * chunk)
 
-    def prepare(hd, s):
-        for c in range(lanes // chunk):
-            qt_v[hd, s, :, lanes_of(c)] = stacked(q_v, hd, s, c).T
-            dot_v[hd, s, :, lanes_of(c)] = stacked(do_v, hd, s, c).T
-
     def probabilities(hd, s):
         psize = plen_ref[rprompt_ref[s]]
         rlen = rlen_ref[s]
@@ -183,7 +178,7 @@
             lax.broadcasted_iota(jnp.int32, (rows, chunk), 1), rows)
         dv = jnp.zeros((all_rows, HEAD_SIZE), F32)
         for c in range(lanes // chunk):
-            scores = dot(keys, qt_v[hd, s, :, lanes_of(c)], NN)
+            scores = dot(keys, stacked(q_v, hd, s, c), NT)
             masked = jnp.concatenate([
                 jnp.where(head_seen, scores[:PLEN], -jnp.inf),
                 jnp.where(tail_seen, scores[PLEN:], -jnp.inf)], axis=0)
@@ -202,7 +197,7 @@
         dk = jnp.zeros((all_rows, HEAD_SIZE), F32)
         for c in range(lanes // chunk):
             prob = p_v[s, :, lanes_of(c)]
-            gprob = dot(values, dot_v[hd, s, :, lanes_of(c)], NN)
+            gprob = dot(values, stacked(do_v, hd, s, c), NT)
             delta = jnp.sum(prob * gprob, axis=0, keepdims=True)
             gscores = (prob * (gprob - delta)).astype(BF16)
             ds_v[hd, s, :, lanes_of(c)] = gscores
@@ -290,19 +285,12 @@
         lax.fori_loop(0, slots, step, 0)
 
     last = slots - 1
-    forward_all(0, 0)
-    forward_all(0, 1)
+    for hd, w in pairs:
+        forward_all(hd, w)
     for load in loads:
         load.wait()
-    each_slot(prepare, 0)
-    for hd, w in pairs[2:]:
-        forward_all(hd, w)
     relay_in(0, 0)
-    for hd in range(1, kvh):
-        each_slot(prepare, hd)
     arrived(0, 0)
-
-    back_steps = []
 
     for hd in range(kvh):
         at = []
@@ -386,7 +374,6 @@
     block = (PLEN, HEAD_SIZE)
     wide = vm((token_rows, q_width), BF16)
     narrow = vm((token_rows, width), BF16)
-    turned = vm((kvh, slots, HEAD_SIZE, lanes), BF16)
     square = (PLEN + rows, lanes)
     per_pair = [
         vm((REACH,) + block, BF16), vm((slots,) + block, F32),
@@ -397,7 +384,7 @@
     scratch = [
         sm(prompt_len.shape, jnp.int32), sm(response_len.shape, jnp.int32),
         sm(response_prompt.shape, jnp.int32),
-        wide, wide, narrow, narrow, turned, turned, vm((slots,) + square, F32),
+        wide, wide, narrow, narrow, vm((slots,) + square, F32),
         vm((kvh, slots) + square, BF16), vm((kvh, slots) + square, BF16),
     ]
     for shape in per_pair:
@@ -423,13 +410,14 @@
         scratch_shapes=scratch,
         compiler_params=pltpu.CompilerParams(
             collective_id=0, has_side_effects=True, vmem_limit_bytes=48 * 1024 * 1024),
-    )(prompt_len, response_len, response_prompt, queries, output_gradient,
-      answer_keys, answer_values, prompt_keys.reshape(span, full),
-      prompt_values.reshape(span, full))
+    )(*[pltpu.with_memory_space_constraint(x, pltpu.HBM) for x in (
+        prompt_len, response_len, response_prompt, queries, output_gradient,
+        answer_keys, answer_values, prompt_keys.reshape(span, full),
+        prompt_values.reshape(span, full))])
     return pl.pallas_call(
         finish,
         out_shape=rows_out + [sds((1, span, full), F32), sds((1, span, full), F32)],
-        in_specs=[anywhere] * 4 + [vmem] * 2,
+        in_specs=[vmem] * 6,
         out_specs=[anywhere] * 6,
         scratch_shapes=[vm((span, full), F32), vm((span, full), F32), dma((6,))],
     )(*results)

time: 132 us -> 55.7 us (0.42)
  the two profiles are of different devices: /device:TPU:1 before, /device:TPU:4 now
where the time goes in v2:
time: 55.7 us; the launch traced here: 55.6 us
  Pallas kernels  50.3 us (90%)
  local copies, waits for them, and re-layouts  4.59 us (8%)
  between operations  0.66 us (1%)
    pallas_call x1, Pallas kernels, on_device(): pl.pallas_call(functools.partial(kernel, (devices, heads, slots, rows, kv...  47 us
    unnamed x12, local copies, waits for them, and re-layouts  4.59 us
    pallas_call x1, Pallas kernels, on_device(): pl.pallas_call(finish, out_shape=rows_out + [sds((1, span, full), F32), s...  3.27 us

profile of v2, /device:TPU:4, one launch (start us, length us, event | category | flops | bytes accessed | tf_op | source)
XLA Modules:
  0.0 55.6 jit_solution(17357966404686850136)
XLA Ops:
  0.6 47.0 %shard_map.136 = (bf16[256,2048]{1,0:T(8,128)(2,1)S(1)}, bf16[256,2048]{1,0:T(8,128)(2,1)S(1)}, bf16[256,256]{1,0:T(8,128)(2,1)S(1)}, bf16[256,256]{1,0:T(8,128)...) custom-call(s32[64]{0:T(128)} %refs_0_.1, s32[4]{0:T(128)} %refs_1_.1, s32[4]{0:T(128)} %refs_2_.1, ...), custom_call_target="tpu_custom_call" | custom-call | tf_op jit(solution)/shard_map/pallas_call | solution.py:405
  47.7 0.0 copy-start
  47.7 1.0 %copy-done = bf16[256,2048]{1,0:T(8,128)(2,1)} copy-done((bf16[256,2048]{1,0:T(8,128)(2,1)}, bf16[256,2048]{1,0:T(8,128)(2,1)S(1)}, u32[]{:S(2)}) %copy-start) | copy-done | bytes 1048600
  48.6 0.0 copy-start.1
  48.7 1.0 %copy-done.1 = bf16[256,2048]{1,0:T(8,128)(2,1)} copy-done((bf16[256,2048]{1,0:T(8,128)(2,1)}, bf16[256,2048]{1,0:T(8,128)(2,1)S(1)}, u32[]{:S(2)}) %copy-start.1) | copy-done | bytes 1048600
  49.7 0.0 copy-start.2
  49.7 0.6 %copy-done.2 = bf16[256,256]{1,0:T(8,128)(2,1)} copy-done((bf16[256,256]{1,0:T(8,128)(2,1)}, bf16[256,256]{1,0:T(8,128)(2,1)S(1)}, u32[]{:S(2)}) %copy-start.2) | copy-done | bytes 131096
  50.3 0.0 copy-start.3
  50.3 0.6 %copy-done.3 = bf16[256,256]{1,0:T(8,128)(2,1)} copy-done((bf16[256,256]{1,0:T(8,128)(2,1)}, bf16[256,256]{1,0:T(8,128)(2,1)S(1)}, u32[]{:S(2)}) %copy-start.3) | copy-done | bytes 131096
  51.0 0.0 copy-start.4
  51.0 0.7 %copy-done.4 = bf16[64,1024]{1,0:T(8,128)(2,1)} copy-done((bf16[64,1024]{1,0:T(8,128)(2,1)}, bf16[64,1024]{1,0:T(8,128)(2,1)S(1)}, u32[]{:S(2)}) %copy-start.4) | copy-done | bytes 131096
  51.6 0.0 copy-start.5
  51.6 0.6 %copy-done.5 = bf16[64,1024]{1,0:T(8,128)(2,1)} copy-done((bf16[64,1024]{1,0:T(8,128)(2,1)}, bf16[64,1024]{1,0:T(8,128)(2,1)S(1)}, u32[]{:S(2)}) %copy-start.5) | copy-done | bytes 131096
  52.3 3.3 %shard_map.137 = (bf16[256,2048]{1,0:T(8,128)(2,1)}, bf16[256,2048]{1,0:T(8,128)(2,1)}, bf16[256,256]{1,0:T(8,128)(2,1)}, bf16[256,256]{1,0:T(8,128)(2,1)}, f32[...) custom-call(bf16[256,2048]{1,0:T(8,128)(2,1)} %copy-done, bf16[256,2048]{1,0:T(8,128)(2,1)} %copy-done.1, ...), custom_call_target="tpu_custom_call" | custom-call | tf_op jit(solution)/shard_map/pallas_call | solution.py:417
Async XLA Ops:
  47.7 1.0 %copy-start = (bf16[256,2048]{1,0:T(8,128)(2,1)}, bf16[256,2048]{1,0:T(8,128)(2,1)S(1)}, u32[]{:S(2)}) copy-start(bf16[256,2048]{1,0:T(8,128)(2,1)S(1)} %get-tuple-element.12.o) | copy-start | bytes 3145732
  48.6 1.0 %copy-start.1 = (bf16[256,2048]{1,0:T(8,128)(2,1)}, bf16[256,2048]{1,0:T(8,128)(2,1)S(1)}, u32[]{:S(2)}) copy-start(bf16[256,2048]{1,0:T(8,128)(2,1)S(1)} %get-tuple-element.13.dq) | copy-start | bytes 3145732
  49.7 0.6 %copy-start.2 = (bf16[256,256]{1,0:T(8,128)(2,1)}, bf16[256,256]{1,0:T(8,128)(2,1)S(1)}, u32[]{:S(2)}) copy-start(bf16[256,256]{1,0:T(8,128)(2,1)S(1)} %get-tuple-element.14.gak) | copy-start | bytes 393220
  50.3 0.6 %copy-start.3 = (bf16[256,256]{1,0:T(8,128)(2,1)}, bf16[256,256]{1,0:T(8,128)(2,1)S(1)}, u32[]{:S(2)}) copy-start(bf16[256,256]{1,0:T(8,128)(2,1)S(1)} %get-tuple-element.15.gav) | copy-start | bytes 393220
  51.0 0.7 %copy-start.4 = (bf16[64,1024]{1,0:T(8,128)(2,1)}, bf16[64,1024]{1,0:T(8,128)(2,1)S(1)}, u32[]{:S(2)}) copy-start(bf16[64,1024]{1,0:T(8,128)(2,1)S(1)} %get-tuple-element.16.gpk) | copy-start | bytes 393220
  51.6 0.6 %copy-start.5 = (bf16[64,1024]{1,0:T(8,128)(2,1)}, bf16[64,1024]{1,0:T(8,128)(2,1)S(1)}, u32[]{:S(2)}) copy-start(bf16[64,1024]{1,0:T(8,128)(2,1)S(1)} %get-tuple-element.17.gpv) | copy-start | bytes 393220

commit v3 on v2

--- a/solution.py
+++ b/solution.py
@@ -47,6 +47,8 @@
     sibling = me + 1 - 2 * core
     up = lax.rem(me + 2, devices)
     down = lax.rem(me + devices - 2, devices)
+    offsets = [-2, 2, -1, 1]
+    near = [lax.rem(me + devices + o, devices) for o in offsets]
     span = PLEN // heads
     width = kvh * HEAD_SIZE
     lanes = group * rows
@@ -82,9 +84,9 @@
     barrier = pltpu.get_barrier_semaphore()
     for p in peers:
         pl.semaphore_signal(barrier, inc=1, device_id={"head": p}, device_id_type=MESH)
-    for d in (sibling, up, down):
+    for d in near:
         pl.semaphore_signal(barrier, inc=1, device_id={"dp": d}, device_id_type=MESH)
-    pl.semaphore_wait(barrier, len(peers) + 3)
+    pl.semaphore_wait(barrier, len(peers) + len(near))
 
     x_in = {}
     for hd, w in pairs:
@@ -97,11 +99,20 @@
                 x_send.at[hd, w, p - 1], x_recv.at[hd, w, p - 1], head=to)
             x_in[hd, w, p].start()
 
+    first_in, last_back = (0, 0), (kvh - 1, 0)
     y_copies, s_copies, r_copies = {}, {}, {}
 
     def forward(hd, w, piece, span_rows):
         ref = kv[hd, w]
         src = ref.at[MAX_SPREAD, span_rows]
+        if (hd, w) == first_in:
+            y_copies[hd, w, piece] = [
+                remote(src, ref.at[MAX_SPREAD - o, span_rows], y_send.at[hd, w, piece, i],
+                       y_recv.at[hd, w, piece, i], dp=near[i]) for i, o in enumerate(offsets)
+            ]
+            for c in y_copies[hd, w, piece]:
+                c.start()
+            return
         y_copies[hd, w, piece] = [
             remote(src, ref.at[0, span_rows], y_send.at[hd, w, piece, 0],
                    y_recv.at[hd, w, piece, 0], dp=up),
@@ -137,6 +148,8 @@
             forward(hd, w, 0, pl.ds(0, PLEN))
 
     def relay_in(hd, w):
+        if (hd, w) == first_in:
+            return
         for p in pieces[hd, w]:
             for c in y_copies[hd, w, p]:
                 c.wait_recv()
@@ -144,11 +157,15 @@
 
     def arrived(hd, w):
         for p in pieces[hd, w]:
+            if (hd, w) == first_in:
+                for c in y_copies[hd, w, p]:
+                    c.wait_recv()
+                continue
             s_copies[hd, w, p].wait_recv()
             r_copies[hd, w, p].wait_recv()
 
     def rows_of(s):
-        return pl.ds(pl.multiple_of(s * rows, rows), rows)
+        return slice(s * rows, (s + 1) * rows)
 
     def columns(hd, c):
         first = hd * group + c * per
@@ -172,10 +189,10 @@
         psize = plen_ref[rprompt_ref[s]]
         rlen = rlen_ref[s]
         keys = both(hd, 0, s)
-        live = (lax.rem(lax.broadcasted_iota(jnp.int32, (1, chunk), 1), rows) < rlen).astype(F32)
+        live = ((lax.broadcasted_iota(jnp.int32, (1, chunk), 1) & (rows - 1)) < rlen).astype(F32)
         head_seen = lax.broadcasted_iota(jnp.int32, (PLEN, chunk), 0) < psize
-        tail_seen = lax.broadcasted_iota(jnp.int32, (rows, chunk), 0) <= lax.rem(
-            lax.broadcasted_iota(jnp.int32, (rows, chunk), 1), rows)
+        tail_seen = lax.broadcasted_iota(jnp.int32, (rows, chunk), 0) <= (
+            lax.broadcasted_iota(jnp.int32, (rows, chunk), 1) & (rows - 1))
         dv = jnp.zeros((all_rows, HEAD_SIZE), F32)
         for c in range(lanes // chunk):
             scores = dot(keys, stacked(q_v, hd, s, c), NT)
@@ -227,9 +244,13 @@
     direct, relayed = 4 * core, 4 - 4 * core
     direct_to = lax.rem(me + devices - 2 + 4 * core, devices)
     relay_to = lax.rem(me + devices + 2 - 4 * core, devices)
-    b_sib, b_direct, b_relay, b_x, b_own = {}, {}, {}, {}, {}
+    b_all, b_sib, b_direct, b_relay, b_x, b_own = {}, {}, {}, {}, {}, {}
     for pair in pairs:
         hd, w = pair
+        b_all[pair] = [
+            remote(y_out[pair].at[i], y_in[pair].at[i], by_send.at[hd, w, i],
+                   by_recv.at[hd, w, i], dp=near[i]) for i in range(len(near))
+        ]
         b_sib[pair] = [
             remote(sib_out[pair].at[i], sib_in[pair].at[i], bs_send.at[hd, w, i],
                    bs_recv.at[hd, w, i], dp=sibling) for i in range(2)
@@ -251,6 +272,12 @@
             x_out[pair].at[mine], dst.at[:, cols], bx_own.at[hd, w])
 
     def back_first(pair):
+        if pair == last_back:
+            for i, o in enumerate(offsets):
+                y_out[pair][i] = summed(pair, MAX_SPREAD + o).astype(BF16)
+                b_all[pair][i].start()
+            own[pair][...] = summed(pair, MAX_SPREAD)
+            return
         for i in range(2):
             sib_out[pair][i] = summed(pair, 1 + 2 * i).astype(BF16)
             b_sib[pair][i].start()
@@ -258,6 +285,8 @@
         b_direct[pair].start()
 
     def back_relay(pair):
+        if pair == last_back:
+            return
         carry = summed(pair, relayed)
         own[pair][...] = summed(pair, MAX_SPREAD)
         for c in b_sib[pair]:
@@ -267,46 +296,42 @@
         own[pair][...] += sib_in[pair][core].astype(F32)
 
     def back_last(pair):
-        b_direct[pair].wait_recv()
-        b_relay[pair].wait_recv()
-        x_out[pair][...] = (own[pair][...] + y_in[pair][0].astype(F32)
-                            + y_in[pair][1].astype(F32)).astype(BF16)
+        came = b_all[pair] if pair == last_back else [b_direct[pair], b_relay[pair]]
+        for c in came:
+            c.wait_recv()
+        total = own[pair][...]
+        for i in range(len(came)):
+            total = total + y_in[pair][i].astype(F32)
+        x_out[pair][...] = total.astype(BF16)
         for c in b_x[pair]:
             c.start()
         b_own[pair].start()
 
     def each_slot(work, hd, at=()):
-        def step(s, carry):
+        for s in range(slots):
             for when, what, *args in at:
-                pl.when(s == when)(functools.partial(what, *args))
+                if when == s:
+                    what(*args)
             work(hd, s)
-            return carry
-
-        lax.fori_loop(0, slots, step, 0)
 
     last = slots - 1
     for hd, w in pairs:
         forward_all(hd, w)
     for load in loads:
         load.wait()
-    relay_in(0, 0)
     arrived(0, 0)
-
     for hd in range(kvh):
         at = []
         if hd == 0:
-            at.append((1, relay_in, 0, 1))
+            at.append((last, relay_in, 0, 1))
         else:
-            at.append((0, back_last, (hd - 1, 1)))
             at.append((1, back_relay, (hd - 1, 0)))
-        if hd + 1 < kvh:
-            at.append((last, relay_in, hd + 1, 0))
         each_slot(probabilities, hd, at)
         back_first((hd, 1))
+        if hd + 1 < kvh:
+            relay_in(hd + 1, 0)
         arrived(hd, 1)
-        at = [(1, back_relay, (hd, 1))]
-        if hd > 0:
-            at.append((0, back_last, (hd - 1, 0)))
+        at = [(min(2, last), back_relay, (hd, 1))]
         if hd + 1 < kvh:
             at.append((last, relay_in, hd + 1, 1))
         each_slot(gradients, hd, at)
@@ -318,9 +343,9 @@
     for hd in range(kvh):
         at = []
         if hd == 0:
-            at = [(1, back_last, (end, 1)), (min(2, last), back_relay, (end, 0))]
+            at += [(1, back_last, pair) for pair in pairs if pair[0] < end]
         if hd == end:
-            at.append((min(2, last), back_last, (end, 0)))
+            at += [(0, back_last, (end, 1)), (1, back_last, (end, 0))]
         each_slot(row_outputs, hd, at)
 
     for pair in pairs:
@@ -328,9 +353,13 @@
         for p in order:
             x_in[hd, w, p].wait_send()
         for p in pieces[pair]:
-            for c in y_copies[hd, w, p] + [s_copies[hd, w, p], r_copies[hd, w, p]]:
+            for c in y_copies[hd, w, p]:
                 c.wait_send()
-        for c in b_sib[pair] + [b_direct[pair], b_relay[pair]]:
+            if pair != first_in:
+                s_copies[hd, w, p].wait_send()
+                r_copies[hd, w, p].wait_send()
+        gone = b_sib[pair] + [b_direct[pair], b_relay[pair]]
+        for c in b_all[pair] if pair == last_back else gone:
             c.wait_send()
         for c in b_x[pair]:
             c.wait()
@@ -378,7 +407,7 @@
     per_pair = [
         vm((REACH,) + block, BF16), vm((slots,) + block, F32),
         vm((2,) + block, BF16), vm((2,) + block, BF16),
-        vm((2,) + block, BF16), vm((2,) + block, BF16),
+        vm((4,) + block, BF16), vm((4,) + block, BF16),
         vm(block, F32), vm(block, BF16),
     ]
     scratch = [
@@ -392,9 +421,9 @@
     scratch += [
         dma((7,)),
         dma((kvh, 2, heads - 1)), dma((kvh, 2, heads - 1)), dma((kvh, 2)),
+        dma((kvh, 2, heads, 4)), dma((kvh, 2, heads, 4)),
         dma((kvh, 2, heads, 2)), dma((kvh, 2, heads, 2)),
-        dma((kvh, 2, heads, 2)), dma((kvh, 2, heads, 2)),
-        dma((kvh, 2, 2)), dma((kvh, 2, 2)), dma((kvh, 2, 2)), dma((kvh, 2, 2)),
+        dma((kvh, 2, 2)), dma((kvh, 2, 2)), dma((kvh, 2, 4)), dma((kvh, 2, 4)),
         dma((kvh, 2, heads - 1)), dma((kvh, 2, heads - 1)), dma((kvh, 2)),
     ]
     sds = jax.ShapeDtypeStruct
@@ -420,7 +449,8 @@
         in_specs=[vmem] * 6,
         out_specs=[anywhere] * 6,
         scratch_shapes=[vm((span, full), F32), vm((span, full), F32), dma((6,))],
-    )(*results)
+        compiler_params=pltpu.CompilerParams(vmem_limit_bytes=4 * 1024 * 1024),
+    )(*[pltpu.with_memory_space_constraint(x, pltpu.VMEM) for x in results])
 
 
 def solution(mesh):

time: 55.7 us -> 41.5 us (0.75)
  the two profiles are of different devices: /device:TPU:4 before, /device:TPU:1 now
where the time goes in v3:
time: 41.5 us; the launch traced here: 41.3 us
  Pallas kernels  40.6 us (98%)
  between operations  0.64 us (2%)
    pallas_call x1, Pallas kernels, on_device(): pl.pallas_call(functools.partial(kernel, (devices, heads, slots, rows, kv...  39 us
    pallas_call x1, Pallas kernels, on_device(): pl.pallas_call(finish, out_shape=rows_out + [sds((1, span, full), F32), s...  1.62 us

profile of v3, /device:TPU:1, one launch (start us, length us, event | category | flops | bytes accessed | tf_op | source)
XLA Modules:
  0.0 41.3 jit_solution(10109020575246860014)
XLA Ops:
  0.6 39.0 %shard_map.136 = (bf16[256,2048]{1,0:T(8,128)(2,1)S(1)}, bf16[256,2048]{1,0:T(8,128)(2,1)S(1)}, bf16[256,256]{1,0:T(8,128)(2,1)S(1)}, bf16[256,256]{1,0:T(8,128)...) custom-call(s32[64]{0:T(128)} %refs_0_.1, s32[4]{0:T(128)} %refs_1_.1, s32[4]{0:T(128)} %refs_2_.1, ...), custom_call_target="tpu_custom_call" | custom-call | tf_op jit(solution)/shard_map/pallas_call | solution.py:434
  39.6 1.6 %shard_map.137 = (bf16[256,2048]{1,0:T(8,128)(2,1)}, bf16[256,2048]{1,0:T(8,128)(2,1)}, bf16[256,256]{1,0:T(8,128)(2,1)}, bf16[256,256]{1,0:T(8,128)(2,1)}, f32[...) custom-call(bf16[256,2048]{1,0:T(8,128)(2,1)S(1)} %get-tuple-element.12.o, bf16[256,2048]{1,0:T(8,128)(2,1)S(1)} %get-tuple-element.13.dq, ...), custom_call_target="tpu_custom_call" | custom-call | tf_op jit(solution)/shard_map/pallas_call | solution.py:446

commit v4 on v3

v4 whole, which is shorter than its diff:
```python
import functools
import math

import jax
import jax.numpy as jnp
from jax import lax
from jax.experimental import pallas as pl
from jax.experimental.pallas import tpu as pltpu
from jax.sharding import PartitionSpec as P

HEAD_SIZE = 128
PLEN = 256
MAX_SPREAD = 2
REACH = 2 * MAX_SPREAD + 1
MESH = pl.DeviceIdType.MESH
SCALING = 1.0 / math.sqrt(HEAD_SIZE)
F32 = jnp.float32
BF16 = jnp.bfloat16


def dot(a, b, dims):
    return lax.dot_general(a, b, (dims, ((), ())), preferred_element_type=F32)


NN = ((1,), (0,))
NT = ((1,), (1,))
TN = ((0,), (0,))


def kernel(sizes, *refs):
    devices, heads, slots, rows, kvh, group = sizes
    pairs = [(hd, w) for hd in range(kvh) for w in range(2)]
    bundles = [[(0, 0)], [(0, 1)]] + [[(hd, 0), (hd, 1)] for hd in range(1, kvh)]
    place = {pair: (b, j) for b, bundle in enumerate(bundles) for j, pair in enumerate(bundle)}
    refs = list(refs)
    (plen_hbm, rlen_hbm, rprompt_hbm, q_hbm, do_hbm, ak_hbm, av_hbm, pk_hbm, pv_hbm,
     o_v, dq_v, gak_v, gav_v, gpk_out, gpv_out,
     plen_ref, rlen_ref, rprompt_ref,
     q_v, do_v, ak_v, av_v, p_v, w_v, ds_v) = refs[:25]
    kv, refs = refs[25:25 + len(bundles)], refs[25 + len(bundles):]
    (part, y_out, y_in, own, x_out) = [
        dict(zip(pairs, refs[i * len(pairs):(i + 1) * len(pairs)])) for i in range(5)
    ]
    (in_sem, x_send, x_recv, x_own, y_send, y_recv,
     by_send, by_recv, bx_send, bx_recv, bx_own) = refs[5 * len(pairs):]

    me = lax.axis_index("dp")
    h = lax.axis_index("head")
    offsets = [-2, 2, -1, 1]
    near = [lax.rem(me + devices + o, devices) for o in offsets]
    span = PLEN // heads
    width = kvh * HEAD_SIZE
    lanes = group * rows
    chunk = min(256, lanes)
    per = chunk // rows
    all_rows = PLEN + rows
    peers = [lax.rem(h + p, heads) for p in range(1, heads)]
    order = [p for p in range(1, heads) if p != heads // 2] + [heads // 2]
    mine = pl.ds(pl.multiple_of(h * span, span), span)

    own_in = {}
    for hd, w in pairs:
        b, j = place[hd, w]
        cols = pl.ds(pl.multiple_of(h * width + hd * HEAD_SIZE, HEAD_SIZE), HEAD_SIZE)
        own_in[hd, w] = pltpu.make_async_copy(
            (pk_hbm, pv_hbm)[w].at[:, cols], kv[b].at[MAX_SPREAD, j, mine], x_own.at[hd, w])
        own_in[hd, w].start()
    loads = [
        pltpu.make_async_copy(src, dst, in_sem.at[i])
        for i, (src, dst) in enumerate(
            [(q_hbm, q_v), (do_hbm, do_v), (ak_hbm, ak_v), (av_hbm, av_v),
             (plen_hbm, plen_ref), (rlen_hbm, rlen_ref), (rprompt_hbm, rprompt_ref)])
    ]
    for load in loads:
        load.start()

    def remote(src, dst, send, recv, **where):
        return pltpu.make_async_remote_copy(
            src_ref=src, dst_ref=dst, send_sem=send, recv_sem=recv,
            device_id=where, device_id_type=MESH)

    barrier = pltpu.get_barrier_semaphore()
    for p in peers:
        pl.semaphore_signal(barrier, inc=1, device_id={"head": p}, device_id_type=MESH)
    for d in near:
        pl.semaphore_signal(barrier, inc=1, device_id={"dp": d}, device_id_type=MESH)
    pl.semaphore_wait(barrier, len(peers) + len(near))

    x_in = {}

    def exchange(hd, w):
        b, j = place[hd, w]
        for p in order:
            to = peers[p - 1]
            cols = pl.ds(pl.multiple_of(to * width + hd * HEAD_SIZE, HEAD_SIZE), HEAD_SIZE)
            x_in[hd, w, p] = remote(
                (pk_hbm, pv_hbm)[w].at[:, cols], kv[b].at[MAX_SPREAD, j, mine],
                x_send.at[hd, w, p - 1], x_recv.at[hd, w, p - 1], head=to)
            x_in[hd, w, p].start()

    y_in_copies = {}

    def forward(b, piece):
        for pair in bundles[b]:
            if piece == 0:
                own_in[pair].wait()
            else:
                x_in[(*pair, piece)].wait_recv()
        source = lax.rem(h + heads - piece, heads)
        at = pl.ds(pl.multiple_of(source * span, span), span)
        for i, o in enumerate(offsets):
            copy = remote(
                kv[b].at[MAX_SPREAD, :, at], kv[b].at[MAX_SPREAD - o, :, at],
                y_send.at[b, piece, i], y_recv.at[b, piece, i], dp=near[i])
            y_in_copies[b, piece, i] = copy
            copy.start()

    def arrived(b):
        for piece in range(heads):
            for i in range(len(near)):
                y_in_copies[b, piece, i].wait_recv()

    exchange(*pairs[0])
    forward(0, 0)
    for pair in pairs[1:]:
        exchange(*pair)
    for b in range(1, len(bundles)):
        forward(b, 0)
    for b in range(len(bundles)):
        for p in order:
            forward(b, p)
    for load in loads:
        load.wait()

    def rows_of(s):
        return slice(s * rows, (s + 1) * rows)

    def columns(hd, c):
        first = hd * group + c * per
        return [slice((first + g) * HEAD_SIZE, (first + g + 1) * HEAD_SIZE) for g in range(per)]

    def stacked(ref, hd, s, c):
        return jnp.concatenate([ref[rows_of(s), col] for col in columns(hd, c)], axis=0)

    def relative(s):
        return lax.rem(rprompt_ref[s] - me + (devices + MAX_SPREAD), devices)

    def both(hd, w, s):
        rel = jnp.minimum(relative(s), REACH - 1)
        tail = (ak_v, av_v)[w][rows_of(s), hd * HEAD_SIZE:(hd + 1) * HEAD_SIZE]
        b, j = place[hd, w]
        return jnp.concatenate([kv[b][rel, j], tail], axis=0)

    def lanes_of(c):
        return slice(c * chunk, (c + 1) * chunk)

    def probabilities(hd, s):
        psize = plen_ref[rprompt_ref[s]]
        rlen = rlen_ref[s]
        keys = both(hd, 0, s)
        live = ((lax.broadcasted_iota(jnp.int32, (1, chunk), 1) & (rows - 1)) < rlen).astype(F32)
        head_seen = lax.broadcasted_iota(jnp.int32, (PLEN, chunk), 0) < psize
        tail_seen = lax.broadcasted_iota(jnp.int32, (rows, chunk), 0) <= (
            lax.broadcasted_iota(jnp.int32, (rows, chunk), 1) & (rows - 1))
        dv = jnp.zeros((all_rows, HEAD_SIZE), F32)
        for c in range(lanes // chunk):
            scores = dot(keys, stacked(q_v, hd, s, c), NT)
            masked = jnp.concatenate([
                jnp.where(head_seen, scores[:PLEN], -jnp.inf),
                jnp.where(tail_seen, scores[PLEN:], -jnp.inf)], axis=0)
            top = jnp.max(masked, axis=0, keepdims=True)
            e = jnp.exp2((masked - top) * (SCALING * math.log2(math.e)))
            prob = e * (live / jnp.sum(e, axis=0, keepdims=True))
            p_v[s, :, lanes_of(c)] = prob
            weights = prob.astype(BF16)
            w_v[hd, s, :, lanes_of(c)] = weights
            dv += dot(weights, stacked(do_v, hd, s, c), NN)
        part[hd, 1][s] = dv[:PLEN]
        gav_v[rows_of(s), hd * HEAD_SIZE:(hd + 1) * HEAD_SIZE] = dv[PLEN:].astype(BF16)

    def gradients(hd, s):
        values = both(hd, 1, s)
        dk = jnp.zeros((all_rows, HEAD_SIZE), F32)
        for c in range(lanes // chunk):
            prob = p_v[s, :, lanes_of(c)]
            gprob = dot(values, stacked(do_v, hd, s, c), NT)
            delta = jnp.sum(prob * gprob, axis=0, keepdims=True)
            gscores = (prob * (gprob - delta)).astype(BF16)
            ds_v[hd, s, :, lanes_of(c)] = gscores
            dk += dot(gscores, stacked(q_v, hd, s, c), NN)
        dk = dk * SCALING
        part[hd, 0][s] = dk[:PLEN]
        gak_v[rows_of(s), hd * HEAD_SIZE:(hd + 1) * HEAD_SIZE] = dk[PLEN:].astype(BF16)

    def row_outputs(hd, s):
        keys_t = both(hd, 0, s).T
        values_t = both(hd, 1, s).T
        for c in range(lanes // chunk):
            out = dot(values_t, w_v[hd, s, :, lanes_of(c)], NN).astype(BF16).T
            dq = (dot(keys_t, ds_v[hd, s, :, lanes_of(c)], NN) * SCALING).astype(BF16).T
            for g, col in enumerate(columns(hd, c)):
                o_v[rows_of(s), col] = out[g * rows:(g + 1) * rows]
                dq_v[rows_of(s), col] = dq[g * rows:(g + 1) * rows]

    def summed(pair, offset):
        total = None
        for s in range(slots):
            pick = jnp.where(relative(s) == offset, 1.0, 0.0).astype(F32)
            term = part[pair][s] * pick
            total = term if total is None else total + term
        return total

    back_y, back_x, back_own = {}, {}, {}
    for hd, w in pairs:
        pair = hd, w
        back_y[pair] = [
            remote(y_out[pair].at[i], y_in[pair].at[i], by_send.at[hd, w, i],
                   by_recv.at[hd, w, i], dp=near[i]) for i in range(len(near))
        ]
        dst = (gpk_out, gpv_out)[w]
        cols = pl.ds(pl.multiple_of(h * width + hd * HEAD_SIZE, HEAD_SIZE), HEAD_SIZE)
        back_x[pair] = []
        for p in order:
            to = peers[p - 1]
            theirs = pl.ds(pl.multiple_of(to * span, span), span)
            back_x[pair].append(remote(
                x_out[pair].at[theirs], dst.at[:, cols],
                bx_send.at[hd, w, p - 1], bx_recv.at[hd, w, p - 1], head=to))
        back_own[pair] = pltpu.make_async_copy(
            x_out[pair].at[mine], dst.at[:, cols], bx_own.at[hd, w])

    def send_back(pair):
        for i, o in enumerate(offsets):
            y_out[pair][i] = summed(pair, MAX_SPREAD + o).astype(BF16)
            back_y[pair][i].start()
        own[pair][...] = summed(pair, MAX_SPREAD)

    def take_back(pair):
        total = own[pair][...]
        for i, copy in enumerate(back_y[pair]):
            copy.wait_recv()
            total = total + y_in[pair][i].astype(F32)
        x_out[pair][...] = total.astype(BF16)
        for copy in back_x[pair]:
            copy.start()
        back_own[pair].start()

    def each_slot(work, hd, at={}):
        for s in range(slots):
            work(hd, s)
            for pair in at.get(s, ()):
                take_back(pair)

    for hd in range(kvh):
        if hd == 0:
            arrived(0)
        else:
            arrived(hd + 1)
        each_slot(probabilities, hd)
        send_back((hd, 1))
        if hd == 0:
            arrived(1)
        each_slot(gradients, hd)
        send_back((hd, 0))

    end = kvh - 1
    for hd in range(kvh):
        if hd < end:
            each_slot(row_outputs, hd, {slots - 1: [(hd, 1), (hd, 0)]})
        else:
            each_slot(row_outputs, hd, {0: [(end, 1)], slots // 2: [(end, 0)]})

    for pair in pairs:
        for p in order:
            x_in[(*pair, p)].wait_send()
        for copy in back_y[pair]:
            copy.wait_send()
        for copy in back_x[pair]:
            copy.wait()
        back_own[pair].wait()
    for copy in y_in_copies.values():
        copy.wait_send()


def finish(o, dq, gak, gav, gpk, gpv, o_out, dq_out, gak_out, gav_out, gpk_out, gpv_out,
           wide_k, wide_v, sem):
    copies = [
        pltpu.make_async_copy(src, dst, sem.at[i])
        for i, (src, dst) in enumerate(
            [(o, o_out), (dq, dq_out), (gak, gak_out), (gav, gav_out),
             (wide_k, gpk_out.at[0]), (wide_v, gpv_out.at[0])])
    ]
    for copy in copies[:4]:
        copy.start()
    wide_k[...] = gpk[...].astype(F32)
    copies[4].start()
    wide_v[...] = gpv[...].astype(F32)
    copies[5].start()
    for copy in copies:
        copy.wait()


def on_device(queries, answer_keys, answer_values, prompt_keys, prompt_values,
              output_gradient, prompt_len, response_len, response_prompt):
    devices, heads = lax.axis_size("dp"), lax.axis_size("head")
    slots = response_len.shape[0]
    token_rows, q_width = queries.shape
    rows = token_rows // slots
    width = answer_keys.shape[1]
    kvh = width // HEAD_SIZE
    group = q_width // width
    lanes = group * rows
    span, full = prompt_keys.shape[1:]
    dma = pltpu.SemaphoreType.DMA
    anywhere = pl.BlockSpec(memory_space=pl.ANY)
    hbm = pl.BlockSpec(memory_space=pltpu.HBM)
    vmem = pl.BlockSpec(memory_space=pltpu.VMEM)
    vm, sm = pltpu.VMEM, pltpu.SMEM
    block = (PLEN, HEAD_SIZE)
    wide = vm((token_rows, q_width), BF16)
    narrow = vm((token_rows, width), BF16)
    square = (PLEN + rows, lanes)
    bundle = [1, 1] + [2] * (kvh - 1)
    scratch = [
        sm(prompt_len.shape, jnp.int32), sm(response_len.shape, jnp.int32),
        sm(response_prompt.shape, jnp.int32),
        wide, wide, narrow, narrow, vm((slots,) + square, F32),
        vm((kvh, slots) + square, BF16), vm((kvh, slots) + square, BF16),
    ]
    scratch += [vm((REACH, count) + block, BF16) for count in bundle]
    for shape in [vm((slots,) + block, F32), vm((REACH - 1,) + block, BF16),
                  vm((REACH - 1,) + block, BF16), vm(block, F32), vm(block, BF16)]:
        scratch += [shape] * (kvh * 2)
    scratch += [
        dma((7,)),
        dma((kvh, 2, heads - 1)), dma((kvh, 2, heads - 1)), dma((kvh, 2)),
        dma((kvh + 1, heads, REACH - 1)), dma((kvh + 1, heads, REACH - 1)),
        dma((kvh, 2, REACH - 1)), dma((kvh, 2, REACH - 1)),
        dma((kvh, 2, heads - 1)), dma((kvh, 2, heads - 1)), dma((kvh, 2)),
    ]
    sds = jax.ShapeDtypeStruct
    rows_out = [
        sds((token_rows, q_width), BF16), sds((token_rows, q_width), BF16),
        sds((token_rows, width), BF16), sds((token_rows, width), BF16),
    ]
    results = pl.pallas_call(
        functools.partial(kernel, (devices, heads, slots, rows, kvh, group)),
        out_shape=rows_out + [sds((span, full), BF16), sds((span, full), BF16)],
        in_specs=[hbm] * 9,
        out_specs=[vmem] * 4 + [anywhere] * 2,
        scratch_shapes=scratch,
        compiler_params=pltpu.CompilerParams(
            collective_id=0, has_side_effects=True, vmem_limit_bytes=48 * 1024 * 1024),
    )(*[pltpu.with_memory_space_constraint(x, pltpu.HBM) for x in (
        prompt_len, response_len, response_prompt, queries, output_gradient,
        answer_keys, answer_values, prompt_keys.reshape(span, full),
        prompt_values.reshape(span, full))])
    return pl.pallas_call(
        finish,
        out_shape=rows_out + [sds((1, span, full), F32), sds((1, span, full), F32)],
        in_specs=[vmem] * 6,
        out_specs=[anywhere] * 6,
        scratch_shapes=[vm((span, full), F32), vm((span, full), F32), dma((6,))],
        compiler_params=pltpu.CompilerParams(vmem_limit_bytes=4 * 1024 * 1024),
    )(*[pltpu.with_memory_space_constraint(x, pltpu.VMEM) for x in results])


def solution(mesh):
    in_specs = (
        P("dp", "head"),
        P("dp", "head"),
        P("dp", "head"),
        P("dp", "head", None),
        P("dp", "head", None),
        P("dp", "head"),
        P(),
        P("dp"),
        P("dp"),
    )
    out_specs = (
        P("dp", "head"),
        P("dp", "head"),
        P("dp", "head"),
        P("dp", "head"),
        P("dp", "head", None),
        P("dp", "head", None),
    )
    return jax.shard_map(
        on_device, mesh=mesh, in_specs=in_specs, out_specs=out_specs, check_vma=False
    )
```

time: 41.5 us -> 39.3 us (0.947)
  Pallas kernels: 40.6 us -> 38.6 us
    pallas_call x1, Pallas kernels: 39 us -> 37 us  [on_device(): pl.pallas_call(functools.partial(kernel, (devices, heads, slots, rows, kv...]
where the time goes in v4:
time: 39.3 us; the launch traced here: 39.2 us
  Pallas kernels  38.6 us (98%)
  between operations  0.64 us (2%)
    pallas_call x1, Pallas kernels, on_device(): pl.pallas_call(functools.partial(kernel, (devices, heads, slots, rows, kv...  37 us
    pallas_call x1, Pallas kernels, on_device(): pl.pallas_call(finish, out_shape=rows_out + [sds((1, span, full), F32), s...  1.62 us

profile of v4, /device:TPU:1, one launch (start us, length us, event | category | flops | bytes accessed | tf_op | source)
XLA Modules:
  0.0 39.2 jit_solution(13045202857915154940)
XLA Ops:
  0.6 37.0 %shard_map.136 = (bf16[256,2048]{1,0:T(8,128)(2,1)S(1)}, bf16[256,2048]{1,0:T(8,128)(2,1)S(1)}, bf16[256,256]{1,0:T(8,128)(2,1)S(1)}, bf16[256,256]{1,0:T(8,128)...) custom-call(s32[64]{0:T(128)} %refs_0_.1, s32[4]{0:T(128)} %refs_1_.1, s32[4]{0:T(128)} %refs_2_.1, ...), custom_call_target="tpu_custom_call" | custom-call | tf_op jit(solution)/shard_map/pallas_call | solution.py:346
  37.6 1.6 %shard_map.137 = (bf16[256,2048]{1,0:T(8,128)(2,1)}, bf16[256,2048]{1,0:T(8,128)(2,1)}, bf16[256,256]{1,0:T(8,128)(2,1)}, bf16[256,256]{1,0:T(8,128)(2,1)}, f32[...) custom-call(bf16[256,2048]{1,0:T(8,128)(2,1)S(1)} %get-tuple-element.12.o, bf16[256,2048]{1,0:T(8,128)(2,1)S(1)} %get-tuple-element.13.dq, ...), custom_call_target="tpu_custom_call" | custom-call | tf_op jit(solution)/shard_map/pallas_call | solution.py:358

commit v5 on v4

--- a/solution.py
+++ b/solution.py
@@ -36,8 +36,8 @@
     (plen_hbm, rlen_hbm, rprompt_hbm, q_hbm, do_hbm, ak_hbm, av_hbm, pk_hbm, pv_hbm,
      o_v, dq_v, gak_v, gav_v, gpk_out, gpv_out,
      plen_ref, rlen_ref, rprompt_ref,
-     q_v, do_v, ak_v, av_v, p_v, w_v, ds_v) = refs[:25]
-    kv, refs = refs[25:25 + len(bundles)], refs[25 + len(bundles):]
+     q_v, do_v, ak_v, av_v, p_v, w_v, ds_v, pk_v, pv_v) = refs[:27]
+    kv, refs = refs[27:27 + len(bundles)], refs[27 + len(bundles):]
     (part, y_out, y_in, own, x_out) = [
         dict(zip(pairs, refs[i * len(pairs):(i + 1) * len(pairs)])) for i in range(5)
     ]
@@ -51,27 +51,24 @@
     span = PLEN // heads
     width = kvh * HEAD_SIZE
     lanes = group * rows
-    chunk = min(256, lanes)
+    chunk = min(512, lanes)
     per = chunk // rows
     all_rows = PLEN + rows
     peers = [lax.rem(h + p, heads) for p in range(1, heads)]
     order = [p for p in range(1, heads) if p != heads // 2] + [heads // 2]
     mine = pl.ds(pl.multiple_of(h * span, span), span)
 
-    own_in = {}
-    for hd, w in pairs:
-        b, j = place[hd, w]
-        cols = pl.ds(pl.multiple_of(h * width + hd * HEAD_SIZE, HEAD_SIZE), HEAD_SIZE)
-        own_in[hd, w] = pltpu.make_async_copy(
-            (pk_hbm, pv_hbm)[w].at[:, cols], kv[b].at[MAX_SPREAD, j, mine], x_own.at[hd, w])
-        own_in[hd, w].start()
+    prompt_loads = [
+        pltpu.make_async_copy(src, dst, x_own.at[i])
+        for i, (src, dst) in enumerate([(pk_hbm, pk_v), (pv_hbm, pv_v)])
+    ]
     loads = [
         pltpu.make_async_copy(src, dst, in_sem.at[i])
         for i, (src, dst) in enumerate(
             [(q_hbm, q_v), (do_hbm, do_v), (ak_hbm, ak_v), (av_hbm, av_v),
              (plen_hbm, plen_ref), (rlen_hbm, rlen_ref), (rprompt_hbm, rprompt_ref)])
     ]
-    for load in loads:
+    for load in prompt_loads + loads:
         load.start()
 
     def remote(src, dst, send, recv, **where):
@@ -84,6 +81,12 @@
         pl.semaphore_signal(barrier, inc=1, device_id={"head": p}, device_id_type=MESH)
     for d in near:
         pl.semaphore_signal(barrier, inc=1, device_id={"dp": d}, device_id_type=MESH)
+    for load in prompt_loads:
+        load.wait()
+    for hd, w in pairs:
+        b, j = place[hd, w]
+        cols = pl.ds(pl.multiple_of(h * width + hd * HEAD_SIZE, HEAD_SIZE), HEAD_SIZE)
+        kv[b][MAX_SPREAD, j, mine] = (pk_v, pv_v)[w][:, cols]
     pl.semaphore_wait(barrier, len(peers) + len(near))
 
     x_in = {}
@@ -94,17 +97,15 @@
             to = peers[p - 1]
             cols = pl.ds(pl.multiple_of(to * width + hd * HEAD_SIZE, HEAD_SIZE), HEAD_SIZE)
             x_in[hd, w, p] = remote(
-                (pk_hbm, pv_hbm)[w].at[:, cols], kv[b].at[MAX_SPREAD, j, mine],
+                (pk_v, pv_v)[w].at[:, cols], kv[b].at[MAX_SPREAD, j, mine],
                 x_send.at[hd, w, p - 1], x_recv.at[hd, w, p - 1], head=to)
             x_in[hd, w, p].start()
 
     y_in_copies = {}
 
     def forward(b, piece):
-        for pair in bundles[b]:
-            if piece == 0:
-                own_in[pair].wait()
-            else:
+        if piece > 0:
+            for pair in bundles[b]:
                 x_in[(*pair, piece)].wait_recv()
         source = lax.rem(h + heads - piece, heads)
         at = pl.ds(pl.multiple_of(source * span, span), span)
@@ -236,14 +237,15 @@
         own[pair][...] = summed(pair, MAX_SPREAD)
 
     def take_back(pair):
-        total = own[pair][...]
-        for i, copy in enumerate(back_y[pair]):
+        for copy in back_y[pair]:
             copy.wait_recv()
-            total = total + y_in[pair][i].astype(F32)
-        x_out[pair][...] = total.astype(BF16)
-        for copy in back_x[pair]:
+        for p, copy in zip(order + [0], back_x[pair] + [back_own[pair]]):
+            at = pl.ds(pl.multiple_of(lax.rem(h + p, heads) * span, span), span)
+            total = own[pair][at]
+            for i in range(len(near)):
+                total = total + y_in[pair][i, at].astype(F32)
+            x_out[pair][at] = total.astype(BF16)
             copy.start()
-        back_own[pair].start()
 
     def each_slot(work, hd, at={}):
         for s in range(slots):
@@ -326,6 +328,7 @@
         sm(response_prompt.shape, jnp.int32),
         wide, wide, narrow, narrow, vm((slots,) + square, F32),
         vm((kvh, slots) + square, BF16), vm((kvh, slots) + square, BF16),
+        vm((span, full), BF16), vm((span, full), BF16),
     ]
     scratch += [vm((REACH, count) + block, BF16) for count in bundle]
     for shape in [vm((slots,) + block, F32), vm((REACH - 1,) + block, BF16),
@@ -333,7 +336,7 @@
         scratch += [shape] * (kvh * 2)
     scratch += [
         dma((7,)),
-        dma((kvh, 2, heads - 1)), dma((kvh, 2, heads - 1)), dma((kvh, 2)),
+        dma((kvh, 2, heads - 1)), dma((kvh, 2, heads - 1)), dma((2,)),
         dma((kvh + 1, heads, REACH - 1)), dma((kvh + 1, heads, REACH - 1)),
         dma((kvh, 2, REACH - 1)), dma((kvh, 2, REACH - 1)),
         dma((kvh, 2, heads - 1)), dma((kvh, 2, heads - 1)), dma((kvh, 2)),

time: 39.3 us -> 39.3 us (level)
  no operation moved by 1% of the time
where the time goes in v5:
time: 39.3 us; the launch traced here: 39.2 us
  Pallas kernels  38.5 us (98%)
  between operations  0.64 us (2%)
    pallas_call x1, Pallas kernels, on_device(): pl.pallas_call(functools.partial(kernel, (devices, heads, slots, rows, kv...  36.9 us
    pallas_call x1, Pallas kernels, on_device(): pl.pallas_call(finish, out_shape=rows_out + [sds((1, span, full), F32), s...  1.62 us

profile of v5, /device:TPU:1, one launch (start us, length us, event | category | flops | bytes accessed | tf_op | source)
XLA Modules:
  0.0 39.2 jit_solution(12017813432628147918)
XLA Ops:
  0.6 36.9 %shard_map.136 = (bf16[256,2048]{1,0:T(8,128)(2,1)S(1)}, bf16[256,2048]{1,0:T(8,128)(2,1)S(1)}, bf16[256,256]{1,0:T(8,128)(2,1)S(1)}, bf16[256,256]{1,0:T(8,128)...) custom-call(s32[64]{0:T(128)} %refs_0_.1, s32[4]{0:T(128)} %refs_1_.1, s32[4]{0:T(128)} %refs_2_.1, ...), custom_call_target="tpu_custom_call" | custom-call | tf_op jit(solution)/shard_map/pallas_call | solution.py:349
  37.5 1.6 %shard_map.137 = (bf16[256,2048]{1,0:T(8,128)(2,1)}, bf16[256,2048]{1,0:T(8,128)(2,1)}, bf16[256,256]{1,0:T(8,128)(2,1)}, bf16[256,256]{1,0:T(8,128)(2,1)}, f32[...) custom-call(bf16[256,2048]{1,0:T(8,128)(2,1)S(1)} %get-tuple-element.12.o, bf16[256,2048]{1,0:T(8,128)(2,1)S(1)} %get-tuple-element.13.dq, ...), custom_call_target="tpu_custom_call" | custom-call | tf_op jit(solution)/shard_map/pallas_call | solution.py:361

commit v6 on v5

--- a/solution.py
+++ b/solution.py
@@ -36,13 +36,13 @@
     (plen_hbm, rlen_hbm, rprompt_hbm, q_hbm, do_hbm, ak_hbm, av_hbm, pk_hbm, pv_hbm,
      o_v, dq_v, gak_v, gav_v, gpk_out, gpv_out,
      plen_ref, rlen_ref, rprompt_ref,
-     q_v, do_v, ak_v, av_v, p_v, w_v, ds_v, pk_v, pv_v) = refs[:27]
-    kv, refs = refs[27:27 + len(bundles)], refs[27 + len(bundles):]
+     q_v, do_v, ak_v, av_v, p_v, w_v, ds_v, pk_v, pv_v, st_v, gt_v) = refs[:29]
+    kv, refs = refs[29:29 + len(bundles)], refs[29 + len(bundles):]
     (part, y_out, y_in, own, x_out) = [
         dict(zip(pairs, refs[i * len(pairs):(i + 1) * len(pairs)])) for i in range(5)
     ]
     (in_sem, x_send, x_recv, x_own, y_send, y_recv,
-     by_send, by_recv, bx_send, bx_recv, bx_own) = refs[5 * len(pairs):]
+     by_send, by_recv, bx_send, bx_recv, bx_own, bl_send, bl_recv) = refs[5 * len(pairs):]
 
     me = lax.axis_index("dp")
     h = lax.axis_index("head")
@@ -51,9 +51,6 @@
     span = PLEN // heads
     width = kvh * HEAD_SIZE
     lanes = group * rows
-    chunk = min(512, lanes)
-    per = chunk // rows
-    all_rows = PLEN + rows
     peers = [lax.rem(h + p, heads) for p in range(1, heads)]
     order = [p for p in range(1, heads) if p != heads // 2] + [heads // 2]
     mine = pl.ds(pl.multiple_of(h * span, span), span)
@@ -121,95 +118,70 @@
             for i in range(len(near)):
                 y_in_copies[b, piece, i].wait_recv()
 
-    exchange(*pairs[0])
-    forward(0, 0)
-    for pair in pairs[1:]:
-        exchange(*pair)
-    for b in range(1, len(bundles)):
-        forward(b, 0)
-    for b in range(len(bundles)):
-        for p in order:
-            forward(b, p)
-    for load in loads:
-        load.wait()
-
     def rows_of(s):
         return slice(s * rows, (s + 1) * rows)
 
-    def columns(hd, c):
-        first = hd * group + c * per
-        return [slice((first + g) * HEAD_SIZE, (first + g + 1) * HEAD_SIZE) for g in range(per)]
-
-    def stacked(ref, hd, s, c):
-        return jnp.concatenate([ref[rows_of(s), col] for col in columns(hd, c)], axis=0)
+    def columns(hd):
+        first = hd * group
+        return [slice((first + g) * HEAD_SIZE, (first + g + 1) * HEAD_SIZE) for g in range(group)]
+
+    def stacked(ref, hd, s):
+        return jnp.concatenate([ref[rows_of(s), col] for col in columns(hd)], axis=0)
 
     def relative(s):
         return lax.rem(rprompt_ref[s] - me + (devices + MAX_SPREAD), devices)
 
-    def both(hd, w, s):
-        rel = jnp.minimum(relative(s), REACH - 1)
-        tail = (ak_v, av_v)[w][rows_of(s), hd * HEAD_SIZE:(hd + 1) * HEAD_SIZE]
+    def prompt_part(hd, w, s):
         b, j = place[hd, w]
-        return jnp.concatenate([kv[b][rel, j], tail], axis=0)
-
-    def lanes_of(c):
-        return slice(c * chunk, (c + 1) * chunk)
+        return kv[b][jnp.minimum(relative(s), REACH - 1), j]
+
+    def answer_part(hd, w, s):
+        return (ak_v, av_v)[w][rows_of(s), hd * HEAD_SIZE:(hd + 1) * HEAD_SIZE]
+
+    def answer_scores(hd, s):
+        seen = lax.broadcasted_iota(jnp.int32, (rows, lanes), 0) <= (
+            lax.broadcasted_iota(jnp.int32, (rows, lanes), 1) & (rows - 1))
+        scores = dot(answer_part(hd, 0, s), stacked(q_v, hd, s), NT)
+        st_v[hd, s] = jnp.where(seen, scores, -jnp.inf)
+        gt_v[hd, s] = dot(answer_part(hd, 1, s), stacked(do_v, hd, s), NT)
 
     def probabilities(hd, s):
         psize = plen_ref[rprompt_ref[s]]
         rlen = rlen_ref[s]
-        keys = both(hd, 0, s)
-        live = ((lax.broadcasted_iota(jnp.int32, (1, chunk), 1) & (rows - 1)) < rlen).astype(F32)
-        head_seen = lax.broadcasted_iota(jnp.int32, (PLEN, chunk), 0) < psize
-        tail_seen = lax.broadcasted_iota(jnp.int32, (rows, chunk), 0) <= (
-            lax.broadcasted_iota(jnp.int32, (rows, chunk), 1) & (rows - 1))
-        dv = jnp.zeros((all_rows, HEAD_SIZE), F32)
-        for c in range(lanes // chunk):
-            scores = dot(keys, stacked(q_v, hd, s, c), NT)
-            masked = jnp.concatenate([
-                jnp.where(head_seen, scores[:PLEN], -jnp.inf),
-                jnp.where(tail_seen, scores[PLEN:], -jnp.inf)], axis=0)
-            top = jnp.max(masked, axis=0, keepdims=True)
-            e = jnp.exp2((masked - top) * (SCALING * math.log2(math.e)))
-            prob = e * (live / jnp.sum(e, axis=0, keepdims=True))
-            p_v[s, :, lanes_of(c)] = prob
-            weights = prob.astype(BF16)
-            w_v[hd, s, :, lanes_of(c)] = weights
-            dv += dot(weights, stacked(do_v, hd, s, c), NN)
-        part[hd, 1][s] = dv[:PLEN]
-        gav_v[rows_of(s), hd * HEAD_SIZE:(hd + 1) * HEAD_SIZE] = dv[PLEN:].astype(BF16)
+        live = ((lax.broadcasted_iota(jnp.int32, (1, lanes), 1) & (rows - 1)) < rlen).astype(F32)
+        seen = lax.broadcasted_iota(jnp.int32, (PLEN, lanes), 0) < psize
+        scores = dot(prompt_part(hd, 0, s), stacked(q_v, hd, s), NT)
+        masked = jnp.concatenate([jnp.where(seen, scores, -jnp.inf), st_v[hd, s]], axis=0)
+        top = jnp.max(masked, axis=0, keepdims=True)
+        e = jnp.exp2((masked - top) * (SCALING * math.log2(math.e)))
+        prob = e * (live / jnp.sum(e, axis=0, keepdims=True))
+        p_v[s] = prob
+        weights = prob.astype(BF16)
+        w_v[hd, s] = weights
+        part[hd, 1][s] = dot(weights[:PLEN], stacked(do_v, hd, s), NN)
 
     def gradients(hd, s):
-        values = both(hd, 1, s)
-        dk = jnp.zeros((all_rows, HEAD_SIZE), F32)
-        for c in range(lanes // chunk):
-            prob = p_v[s, :, lanes_of(c)]
-            gprob = dot(values, stacked(do_v, hd, s, c), NT)
-            delta = jnp.sum(prob * gprob, axis=0, keepdims=True)
-            gscores = (prob * (gprob - delta)).astype(BF16)
-            ds_v[hd, s, :, lanes_of(c)] = gscores
-            dk += dot(gscores, stacked(q_v, hd, s, c), NN)
-        dk = dk * SCALING
-        part[hd, 0][s] = dk[:PLEN]
-        gak_v[rows_of(s), hd * HEAD_SIZE:(hd + 1) * HEAD_SIZE] = dk[PLEN:].astype(BF16)
+        prob = p_v[s]
+        gprob = jnp.concatenate([
+            dot(prompt_part(hd, 1, s), stacked(do_v, hd, s), NT), gt_v[hd, s]], axis=0)
+        delta = jnp.sum(prob * gprob, axis=0, keepdims=True)
+        gscores = (prob * (gprob - delta)).astype(BF16)
+        ds_v[hd, s] = gscores
+        part[hd, 0][s] = dot(gscores[:PLEN], stacked(q_v, hd, s), NN) * SCALING
 
     def row_outputs(hd, s):
-        keys_t = both(hd, 0, s).T
-        values_t = both(hd, 1, s).T
-        for c in range(lanes // chunk):
-            out = dot(values_t, w_v[hd, s, :, lanes_of(c)], NN).astype(BF16).T
-            dq = (dot(keys_t, ds_v[hd, s, :, lanes_of(c)], NN) * SCALING).astype(BF16).T
-            for g, col in enumerate(columns(hd, c)):
-                o_v[rows_of(s), col] = out[g * rows:(g + 1) * rows]
-                dq_v[rows_of(s), col] = dq[g * rows:(g + 1) * rows]
-
-    def summed(pair, offset):
-        total = None
-        for s in range(slots):
-            pick = jnp.where(relative(s) == offset, 1.0, 0.0).astype(F32)
-            term = part[pair][s] * pick
-            total = term if total is None else total + term
-        return total
+        keys_t = jnp.concatenate([prompt_part(hd, 0, s), answer_part(hd, 0, s)], axis=0).T
+        values_t = jnp.concatenate([prompt_part(hd, 1, s), answer_part(hd, 1, s)], axis=0).T
+        out = dot(values_t, w_v[hd, s], NN).astype(BF16).T
+        dq = (dot(keys_t, ds_v[hd, s], NN) * SCALING).astype(BF16).T
+        for g, col in enumerate(columns(hd)):
+            o_v[rows_of(s), col] = out[g * rows:(g + 1) * rows]
+            dq_v[rows_of(s), col] = dq[g * rows:(g + 1) * rows]
+        cols = slice(hd * HEAD_SIZE, (hd + 1) * HEAD_SIZE)
+        gav_v[rows_of(s), cols] = dot(
+            w_v[hd, s, PLEN:], stacked(do_v, hd, s), NN).astype(BF16)
+        gak_v[rows_of(s), cols] = (dot(
+            ds_v[hd, s, PLEN:], stacked(q_v, hd, s), NN) * SCALING).astype(BF16)
 
     back_y, back_x, back_own = {}, {}, {}
     for hd, w in pairs:
@@ -230,34 +202,76 @@
         back_own[pair] = pltpu.make_async_copy(
             x_out[pair].at[mine], dst.at[:, cols], bx_own.at[hd, w])
 
+    last = kvh - 1, 0
+    back_last = {}
+    for p in range(heads):
+        at = pl.ds(pl.multiple_of(lax.rem(h + p, heads) * span, span), span)
+        for i in range(len(near)):
+            back_last[p, i] = remote(
+                y_out[last].at[i, at], y_in[last].at[i, at], bl_send.at[p, i],
+                bl_recv.at[p, i], dp=near[i])
+
+    def block_rows(p):
+        return pl.ds(pl.multiple_of(lax.rem(h + p, heads) * span, span), span)
+
     def send_back(pair):
-        for i, o in enumerate(offsets):
-            y_out[pair][i] = summed(pair, MAX_SPREAD + o).astype(BF16)
-            back_y[pair][i].start()
-        own[pair][...] = summed(pair, MAX_SPREAD)
+        for p in order + [0]:
+            at = block_rows(p)
+            terms = [part[pair][s, at] for s in range(slots)]
+            for i, o in enumerate(offsets + [0]):
+                total = None
+                for s in range(slots):
+                    term = terms[s] * picks[s, o]
+                    total = term if total is None else total + term
+                if o == 0:
+                    own[pair][at] = total
+                else:
+                    y_out[pair][i, at] = total.astype(BF16)
+                    if pair == last:
+                        back_last[p, i].start()
+        if pair != last:
+            for copy in back_y[pair]:
+                copy.start()
 
     def take_back(pair):
-        for copy in back_y[pair]:
-            copy.wait_recv()
+        if pair != last:
+            for copy in back_y[pair]:
+                copy.wait_recv()
         for p, copy in zip(order + [0], back_x[pair] + [back_own[pair]]):
-            at = pl.ds(pl.multiple_of(lax.rem(h + p, heads) * span, span), span)
+            at = block_rows(p)
             total = own[pair][at]
             for i in range(len(near)):
+                if pair == last:
+                    back_last[p, i].wait_recv()
                 total = total + y_in[pair][i, at].astype(F32)
             x_out[pair][at] = total.astype(BF16)
             copy.start()
 
-    def each_slot(work, hd, at={}):
+    def each_slot(work, hd):
         for s in range(slots):
             work(hd, s)
-            for pair in at.get(s, ()):
-                take_back(pair)
+
+    exchange(*pairs[0])
+    forward(0, 0)
+    for pair in pairs[1:]:
+        exchange(*pair)
+    for b in range(1, len(bundles)):
+        forward(b, 0)
+    for load in loads:
+        load.wait()
+    picks = {
+        (s, o): jnp.where(relative(s) == MAX_SPREAD + o, 1.0, 0.0).astype(F32)
+        for s in range(slots) for o in offsets + [0]
+    }
+    each_slot(answer_scores, 0)
+    for b in range(len(bundles)):
+        for p in order:
+            forward(b, p)
+    for hd in range(1, kvh):
+        each_slot(answer_scores, hd)
 
     for hd in range(kvh):
-        if hd == 0:
-            arrived(0)
-        else:
-            arrived(hd + 1)
+        arrived(hd + 1 if hd > 0 else 0)
         each_slot(probabilities, hd)
         send_back((hd, 1))
         if hd == 0:
@@ -265,22 +279,26 @@
         each_slot(gradients, hd)
         send_back((hd, 0))
 
-    end = kvh - 1
-    for hd in range(kvh):
-        if hd < end:
-            each_slot(row_outputs, hd, {slots - 1: [(hd, 1), (hd, 0)]})
-        else:
-            each_slot(row_outputs, hd, {0: [(end, 1)], slots // 2: [(end, 0)]})
+    for hd in range(kvh - 1):
+        each_slot(row_outputs, hd)
+        take_back((hd, 1))
+        take_back((hd, 0))
+    take_back((kvh - 1, 1))
+    row_outputs(kvh - 1, 0)
+    take_back(last)
+    for s in range(1, slots):
+        row_outputs(kvh - 1, s)
 
     for pair in pairs:
         for p in order:
             x_in[(*pair, p)].wait_send()
-        for copy in back_y[pair]:
-            copy.wait_send()
+        if pair != last:
+            for copy in back_y[pair]:
+                copy.wait_send()
         for copy in back_x[pair]:
             copy.wait()
         back_own[pair].wait()
-    for copy in y_in_copies.values():
+    for copy in [*y_in_copies.values(), *back_last.values()]:
         copy.wait_send()
 
 
@@ -329,6 +347,7 @@
         wide, wide, narrow, narrow, vm((slots,) + square, F32),
         vm((kvh, slots) + square, BF16), vm((kvh, slots) + square, BF16),
         vm((span, full), BF16), vm((span, full), BF16),
+        vm((kvh, slots, rows, lanes), F32), vm((kvh, slots, rows, lanes), F32),
     ]
     scratch += [vm((REACH, count) + block, BF16) for count in bundle]
     for shape in [vm((slots,) + block, F32), vm((REACH - 1,) + block, BF16),
@@ -340,6 +359,7 @@
         dma((kvh + 1, heads, REACH - 1)), dma((kvh + 1, heads, REACH - 1)),
         dma((kvh, 2, REACH - 1)), dma((kvh, 2, REACH - 1)),
         dma((kvh, 2, heads - 1)), dma((kvh, 2, heads - 1)), dma((kvh, 2)),
+        dma((heads, REACH - 1)), dma((heads, REACH - 1)),
     ]
     sds = jax.ShapeDtypeStruct
     rows_out = [

time: 39.3 us -> 40 us (1.018)
  Pallas kernels: 38.5 us -> 39.2 us
    pallas_call x1, Pallas kernels: 36.9 us -> 37.6 us  [on_device(): pl.pallas_call(functools.partial(kernel, (devices, heads, slots, rows, kv...]
where the time goes in v6:
time: 40 us; the launch traced here: 39.9 us
  Pallas kernels  39.2 us (98%)
  between operations  0.64 us (2%)
    pallas_call x1, Pallas kernels, on_device(): pl.pallas_call(functools.partial(kernel, (devices, heads, slots, rows, kv...  37.6 us
    pallas_call x1, Pallas kernels, on_device(): pl.pallas_call(finish, out_shape=rows_out + [sds((1, span, full), F32), s...  1.62 us

profile of v6, /device:TPU:1, one launch (start us, length us, event | category | flops | bytes accessed | tf_op | source)
XLA Modules:
  0.0 39.9 jit_solution(4389992521212735164)
XLA Ops:
  0.6 37.6 %shard_map.136 = (bf16[256,2048]{1,0:T(8,128)(2,1)S(1)}, bf16[256,2048]{1,0:T(8,128)(2,1)S(1)}, bf16[256,256]{1,0:T(8,128)(2,1)S(1)}, bf16[256,256]{1,0:T(8,128)...) custom-call(s32[64]{0:T(128)} %refs_0_.1, s32[4]{0:T(128)} %refs_1_.1, s32[4]{0:T(128)} %refs_2_.1, ...), custom_call_target="tpu_custom_call" | custom-call | tf_op jit(solution)/shard_map/pallas_call | solution.py:369
  38.2 1.6 %shard_map.137 = (bf16[256,2048]{1,0:T(8,128)(2,1)}, bf16[256,2048]{1,0:T(8,128)(2,1)}, bf16[256,256]{1,0:T(8,128)(2,1)}, bf16[256,256]{1,0:T(8,128)(2,1)}, f32[...) custom-call(bf16[256,2048]{1,0:T(8,128)(2,1)S(1)} %get-tuple-element.12.o, bf16[256,2048]{1,0:T(8,128)(2,1)S(1)} %get-tuple-element.13.dq, ...), custom_call_target="tpu_custom_call" | custom-call | tf_op jit(solution)/shard_map/pallas_call | solution.py:381

commit v7 on v6

--- a/solution.py
+++ b/solution.py
@@ -271,6 +271,8 @@
         each_slot(answer_scores, hd)
 
     for hd in range(kvh):
+        if hd > 0:
+            each_slot(row_outputs, hd - 1)
         arrived(hd + 1 if hd > 0 else 0)
         each_slot(probabilities, hd)
         send_back((hd, 1))
@@ -280,13 +282,14 @@
         send_back((hd, 0))
 
     for hd in range(kvh - 1):
-        each_slot(row_outputs, hd)
         take_back((hd, 1))
         take_back((hd, 0))
+    row_outputs(kvh - 1, 0)
+    row_outputs(kvh - 1, 1)
     take_back((kvh - 1, 1))
-    row_outputs(kvh - 1, 0)
+    row_outputs(kvh - 1, 2)
     take_back(last)
-    for s in range(1, slots):
+    for s in range(3, slots):
         row_outputs(kvh - 1, s)
 
     for pair in pairs:

time: 40 us -> 40.4 us (1.010)
  Pallas kernels: 39.2 us -> 39.7 us
    pallas_call x1, Pallas kernels: 37.6 us -> 38.1 us  [on_device(): pl.pallas_call(functools.partial(kernel, (devices, heads, slots, rows, kv...]
where the time goes in v7:
time: 40.4 us; the launch traced here: 40.3 us
  Pallas kernels  39.7 us (98%)
  between operations  0.64 us (2%)
    pallas_call x1, Pallas kernels, on_device(): pl.pallas_call(functools.partial(kernel, (devices, heads, slots, rows, kv...  38.1 us
    pallas_call x1, Pallas kernels, on_device(): pl.pallas_call(finish, out_shape=rows_out + [sds((1, span, full), F32), s...  1.62 us

profile of v7, /device:TPU:1, one launch (start us, length us, event | category | flops | bytes accessed | tf_op | source)
XLA Modules:
  0.0 40.3 jit_solution(2856305895172220393)
XLA Ops:
  0.6 38.1 %shard_map.136 = (bf16[256,2048]{1,0:T(8,128)(2,1)S(1)}, bf16[256,2048]{1,0:T(8,128)(2,1)S(1)}, bf16[256,256]{1,0:T(8,128)(2,1)S(1)}, bf16[256,256]{1,0:T(8,128)...) custom-call(s32[64]{0:T(128)} %refs_0_.1, s32[4]{0:T(128)} %refs_1_.1, s32[4]{0:T(128)} %refs_2_.1, ...), custom_call_target="tpu_custom_call" | custom-call | tf_op jit(solution)/shard_map/pallas_call | solution.py:372
  38.7 1.6 %shard_map.137 = (bf16[256,2048]{1,0:T(8,128)(2,1)}, bf16[256,2048]{1,0:T(8,128)(2,1)}, bf16[256,256]{1,0:T(8,128)(2,1)}, bf16[256,256]{1,0:T(8,128)(2,1)}, f32[...) custom-call(bf16[256,2048]{1,0:T(8,128)(2,1)S(1)} %get-tuple-element.12.o, bf16[256,2048]{1,0:T(8,128)(2,1)S(1)} %get-tuple-element.13.dq, ...), custom_call_target="tpu_custom_call" | custom-call | tf_op jit(solution)/shard_map/pallas_call | solution.py:384

commit v8 on v6

--- a/solution.py
+++ b/solution.py
@@ -12,6 +12,7 @@
 PLEN = 256
 MAX_SPREAD = 2
 REACH = 2 * MAX_SPREAD + 1
+SIDE = 256
 MESH = pl.DeviceIdType.MESH
 SCALING = 1.0 / math.sqrt(HEAD_SIZE)
 F32 = jnp.float32
@@ -36,8 +37,8 @@
     (plen_hbm, rlen_hbm, rprompt_hbm, q_hbm, do_hbm, ak_hbm, av_hbm, pk_hbm, pv_hbm,
      o_v, dq_v, gak_v, gav_v, gpk_out, gpv_out,
      plen_ref, rlen_ref, rprompt_ref,
-     q_v, do_v, ak_v, av_v, p_v, w_v, ds_v, pk_v, pv_v, st_v, gt_v) = refs[:29]
-    kv, refs = refs[29:29 + len(bundles)], refs[29 + len(bundles):]
+     q_v, do_v, ak_v, av_v, p_v, w_v, ds_v, pk_v, pv_v, st_v, gt_v, id_v) = refs[:30]
+    kv, refs = refs[30:30 + len(bundles)], refs[30 + len(bundles):]
     (part, y_out, y_in, own, x_out) = [
         dict(zip(pairs, refs[i * len(pairs):(i + 1) * len(pairs)])) for i in range(5)
     ]
@@ -78,6 +79,8 @@
         pl.semaphore_signal(barrier, inc=1, device_id={"head": p}, device_id_type=MESH)
     for d in near:
         pl.semaphore_signal(barrier, inc=1, device_id={"dp": d}, device_id_type=MESH)
+    id_v[...] = (lax.broadcasted_iota(jnp.int32, (SIDE, SIDE), 0)
+                 == lax.broadcasted_iota(jnp.int32, (SIDE, SIDE), 1)).astype(F32).astype(BF16)
     for load in prompt_loads:
         load.wait()
     for hd, w in pairs:
@@ -169,14 +172,22 @@
         ds_v[hd, s] = gscores
         part[hd, 0][s] = dot(gscores[:PLEN], stacked(q_v, hd, s), NN) * SCALING
 
+    def turned(x):
+        side = x.shape[1]
+        return dot(id_v[:side, :side], x, NT).astype(BF16)
+
     def row_outputs(hd, s):
-        keys_t = jnp.concatenate([prompt_part(hd, 0, s), answer_part(hd, 0, s)], axis=0).T
-        values_t = jnp.concatenate([prompt_part(hd, 1, s), answer_part(hd, 1, s)], axis=0).T
-        out = dot(values_t, w_v[hd, s], NN).astype(BF16).T
-        dq = (dot(keys_t, ds_v[hd, s], NN) * SCALING).astype(BF16).T
-        for g, col in enumerate(columns(hd)):
-            o_v[rows_of(s), col] = out[g * rows:(g + 1) * rows]
-            dq_v[rows_of(s), col] = dq[g * rows:(g + 1) * rows]
+        keys = jnp.concatenate([prompt_part(hd, 0, s), answer_part(hd, 0, s)], axis=0)
+        values = jnp.concatenate([prompt_part(hd, 1, s), answer_part(hd, 1, s)], axis=0)
+        out = dot(turned(values), w_v[hd, s], NN).astype(BF16)
+        dq = (dot(turned(keys), ds_v[hd, s], NN) * SCALING).astype(BF16)
+        per = SIDE // rows
+        for c in range(lanes // SIDE):
+            out_rows = turned(out[:, c * SIDE:(c + 1) * SIDE])
+            dq_rows = turned(dq[:, c * SIDE:(c + 1) * SIDE])
+            for g, col in enumerate(columns(hd)[c * per:(c + 1) * per]):
+                o_v[rows_of(s), col] = out_rows[g * rows:(g + 1) * rows]
+                dq_v[rows_of(s), col] = dq_rows[g * rows:(g + 1) * rows]
         cols = slice(hd * HEAD_SIZE, (hd + 1) * HEAD_SIZE)
         gav_v[rows_of(s), cols] = dot(
             w_v[hd, s, PLEN:], stacked(do_v, hd, s), NN).astype(BF16)
@@ -348,6 +359,7 @@
         vm((kvh, slots) + square, BF16), vm((kvh, slots) + square, BF16),
         vm((span, full), BF16), vm((span, full), BF16),
         vm((kvh, slots, rows, lanes), F32), vm((kvh, slots, rows, lanes), F32),
+        vm((SIDE, SIDE), BF16),
     ]
     scratch += [vm((REACH, count) + block, BF16) for count in bundle]
     for shape in [vm((slots,) + block, F32), vm((REACH - 1,) + block, BF16),

time: 40 us -> 40.1 us (level)
  no operation moved by 1% of the time
where the time goes in v8:
time: 40.1 us; the launch traced here: 40 us
  Pallas kernels  39.3 us (98%)
  between operations  0.64 us (2%)
    pallas_call x1, Pallas kernels, on_device(): pl.pallas_call(functools.partial(kernel, (devices, heads, slots, rows, kv...  37.7 us
    pallas_call x1, Pallas kernels, on_device(): pl.pallas_call(finish, out_shape=rows_out + [sds((1, span, full), F32), s...  1.62 us

profile of v8, /device:TPU:1, one launch (start us, length us, event | category | flops | bytes accessed | tf_op | source)
XLA Modules:
  0.0 40.0 jit_solution(1159159813092977921)
XLA Ops:
  0.6 37.7 %shard_map.136 = (bf16[256,2048]{1,0:T(8,128)(2,1)S(1)}, bf16[256,2048]{1,0:T(8,128)(2,1)S(1)}, bf16[256,256]{1,0:T(8,128)(2,1)S(1)}, bf16[256,256]{1,0:T(8,128)...) custom-call(s32[64]{0:T(128)} %refs_0_.1, s32[4]{0:T(128)} %refs_1_.1, s32[4]{0:T(128)} %refs_2_.1, ...), custom_call_target="tpu_custom_call" | custom-call | tf_op jit(solution)/shard_map/pallas_call | solution.py:381
  38.3 1.6 %shard_map.137 = (bf16[256,2048]{1,0:T(8,128)(2,1)}, bf16[256,2048]{1,0:T(8,128)(2,1)}, bf16[256,256]{1,0:T(8,128)(2,1)}, bf16[256,256]{1,0:T(8,128)(2,1)}, f32[...) custom-call(bf16[256,2048]{1,0:T(8,128)(2,1)S(1)} %get-tuple-element.12.o, bf16[256,2048]{1,0:T(8,128)(2,1)S(1)} %get-tuple-element.13.dq, ...), custom_call_target="tpu_custom_call" | custom-call | tf_op jit(solution)/shard_map/pallas_call | solution.py:393

commit v9 on v6

v9 whole, which is shorter than its diff:
```python
import functools
import math

import jax
import jax.numpy as jnp
from jax import lax
from jax.experimental import pallas as pl
from jax.experimental.pallas import tpu as pltpu
from jax.sharding import PartitionSpec as P

HEAD_SIZE = 128
PLEN = 256
MAX_SPREAD = 2
REACH = 2 * MAX_SPREAD + 1
MESH = pl.DeviceIdType.MESH
SCALING = 1.0 / math.sqrt(HEAD_SIZE)
F32 = jnp.float32
BF16 = jnp.bfloat16


def dot(a, b, dims):
    return lax.dot_general(a, b, (dims, ((), ())), preferred_element_type=F32)


NN = ((1,), (0,))
NT = ((1,), (1,))
TN = ((0,), (0,))


def kernel(sizes, *refs):
    devices, heads, slots, rows, kvh, group = sizes
    span = PLEN // heads
    width = kvh * HEAD_SIZE
    lanes = group * rows
    inward = [(0, 0, kvh)] + [(1, hd, 1) for hd in range(kvh)]
    outward = [(1, 0, kvh)] + [(0, hd, 1) for hd in range(kvh)]
    refs = list(refs)
    (plen_hbm, rlen_hbm, rprompt_hbm, q_hbm, do_hbm, ak_hbm, av_hbm, pk_hbm, pv_hbm,
     o_v, dq_v, gak_v, gav_v, gpk_out, gpv_out,
     plen_ref, rlen_ref, rprompt_ref,
     q_v, do_v, ak_v, av_v, p_v, w_v, ds_v, pk_v, pv_v, st_v, gt_v) = refs[:29]
    kv, refs = refs[29:29 + len(inward)], refs[29 + len(inward):]
    (part, y_out, y_in, own, x_out) = [
        refs[i * len(outward):(i + 1) * len(outward)] for i in range(5)
    ]
    (in_sem, x_send, x_recv, x_own, y_send, y_recv,
     by_send, by_recv, bx_send, bx_recv, bx_own) = refs[5 * len(outward):]

    me = lax.axis_index("dp")
    h = lax.axis_index("head")
    offsets = [-2, 2, -1, 1]
    near = [lax.rem(me + devices + o, devices) for o in offsets]
    peers = [lax.rem(h + p, heads) for p in range(1, heads)]
    order = [p for p in range(1, heads) if p != heads // 2] + [heads // 2]
    mine = pl.ds(pl.multiple_of(h * span, span), span)

    prompt_loads = [
        pltpu.make_async_copy(src, dst, x_own.at[i])
        for i, (src, dst) in enumerate([(pk_hbm, pk_v), (pv_hbm, pv_v)])
    ]
    loads = [
        pltpu.make_async_copy(src, dst, in_sem.at[i])
        for i, (src, dst) in enumerate(
            [(q_hbm, q_v), (do_hbm, do_v), (ak_hbm, ak_v), (av_hbm, av_v),
             (plen_hbm, plen_ref), (rlen_hbm, rlen_ref), (rprompt_hbm, rprompt_ref)])
    ]
    for load in prompt_loads + loads:
        load.start()

    def remote(src, dst, send, recv, **where):
        return pltpu.make_async_remote_copy(
            src_ref=src, dst_ref=dst, send_sem=send, recv_sem=recv,
            device_id=where, device_id_type=MESH)

    def columns_at(holder, hd, count):
        return pl.ds(
            pl.multiple_of(holder * width + hd * HEAD_SIZE, HEAD_SIZE), count * HEAD_SIZE)

    barrier = pltpu.get_barrier_semaphore()
    for p in peers:
        pl.semaphore_signal(barrier, inc=1, device_id={"head": p}, device_id_type=MESH)
    for d in near:
        pl.semaphore_signal(barrier, inc=1, device_id={"dp": d}, device_id_type=MESH)
    for load in prompt_loads:
        load.wait()
    for b, (w, hd, count) in enumerate(inward):
        kv[b][MAX_SPREAD, mine] = (pk_v, pv_v)[w][:, columns_at(h, hd, count)]
    pl.semaphore_wait(barrier, len(peers) + len(near))

    x_in = {}

    def exchange(b):
        w, hd, count = inward[b]
        for p in order:
            to = peers[p - 1]
            x_in[b, p] = remote(
                (pk_v, pv_v)[w].at[:, columns_at(to, hd, count)], kv[b].at[MAX_SPREAD, mine],
                x_send.at[b, p - 1], x_recv.at[b, p - 1], head=to)
            x_in[b, p].start()

    y_in_copies = {}

    def to_neighbours(b, piece, at):
        for i, o in enumerate(offsets):
            copy = remote(
                kv[b].at[MAX_SPREAD, at], kv[b].at[MAX_SPREAD - o, at],
                y_send.at[b, piece, i], y_recv.at[b, piece, i], dp=near[i])
            y_in_copies[b, piece, i] = copy
            copy.start()

    def forward(b, piece):
        if piece > 0:
            x_in[b, piece].wait_recv()
        source = lax.rem(h + heads - piece, heads)
        to_neighbours(b, piece, pl.ds(pl.multiple_of(source * span, span), span))

    def forward_whole(b):
        for p in order:
            x_in[b, p].wait_recv()
        to_neighbours(b, 0, pl.ds(0, PLEN))

    def arrived(b):
        for key, copy in y_in_copies.items():
            if key[0] == b:
                copy.wait_recv()

    def rows_of(s):
        return slice(s * rows, (s + 1) * rows)

    def columns(hd):
        first = hd * group
        return [slice((first + g) * HEAD_SIZE, (first + g + 1) * HEAD_SIZE) for g in range(group)]

    def stacked(ref, hd, s):
        return jnp.concatenate([ref[rows_of(s), col] for col in columns(hd)], axis=0)

    def relative(s):
        return lax.rem(rprompt_ref[s] - me + (devices + MAX_SPREAD), devices)

    def prompt_part(hd, w, s):
        rel = jnp.minimum(relative(s), REACH - 1)
        if w == 1:
            return kv[1 + hd][rel]
        return kv[0][rel, :, hd * HEAD_SIZE:(hd + 1) * HEAD_SIZE]

    def answer_part(hd, w, s):
        return (ak_v, av_v)[w][rows_of(s), hd * HEAD_SIZE:(hd + 1) * HEAD_SIZE]

    def answer_scores(hd, s):
        seen = lax.broadcasted_iota(jnp.int32, (rows, lanes), 0) <= (
            lax.broadcasted_iota(jnp.int32, (rows, lanes), 1) & (rows - 1))
        scores = dot(answer_part(hd, 0, s), stacked(q_v, hd, s), NT)
        st_v[hd, s] = jnp.where(seen, scores, -jnp.inf)
        gt_v[hd, s] = dot(answer_part(hd, 1, s), stacked(do_v, hd, s), NT)

    def probabilities(hd, s):
        psize = plen_ref[rprompt_ref[s]]
        rlen = rlen_ref[s]
        live = ((lax.broadcasted_iota(jnp.int32, (1, lanes), 1) & (rows - 1)) < rlen).astype(F32)
        seen = lax.broadcasted_iota(jnp.int32, (PLEN, lanes), 0) < psize
        scores = dot(prompt_part(hd, 0, s), stacked(q_v, hd, s), NT)
        masked = jnp.concatenate([jnp.where(seen, scores, -jnp.inf), st_v[hd, s]], axis=0)
        top = jnp.max(masked, axis=0, keepdims=True)
        e = jnp.exp2((masked - top) * (SCALING * math.log2(math.e)))
        prob = e * (live / jnp.sum(e, axis=0, keepdims=True))
        p_v[hd, s] = prob
        weights = prob.astype(BF16)
        w_v[hd, s] = weights
        part[0][s, :, hd * HEAD_SIZE:(hd + 1) * HEAD_SIZE] = dot(
            weights[:PLEN], stacked(do_v, hd, s), NN)

    def gradients(hd, s):
        prob = p_v[hd, s]
        gprob = jnp.concatenate([
            dot(prompt_part(hd, 1, s), stacked(do_v, hd, s), NT), gt_v[hd, s]], axis=0)
        delta = jnp.sum(prob * gprob, axis=0, keepdims=True)
        gscores = (prob * (gprob - delta)).astype(BF16)
        ds_v[hd, s] = gscores
        part[1 + hd][s] = dot(gscores[:PLEN], stacked(q_v, hd, s), NN) * SCALING

    def row_outputs(hd, s):
        keys_t = jnp.concatenate([prompt_part(hd, 0, s), answer_part(hd, 0, s)], axis=0).T
        values_t = jnp.concatenate([prompt_part(hd, 1, s), answer_part(hd, 1, s)], axis=0).T
        out = dot(values_t, w_v[hd, s], NN).astype(BF16).T
        dq = (dot(keys_t, ds_v[hd, s], NN) * SCALING).astype(BF16).T
        for g, col in enumerate(columns(hd)):
            o_v[rows_of(s), col] = out[g * rows:(g + 1) * rows]
            dq_v[rows_of(s), col] = dq[g * rows:(g + 1) * rows]
        cols = slice(hd * HEAD_SIZE, (hd + 1) * HEAD_SIZE)
        gav_v[rows_of(s), cols] = dot(
            w_v[hd, s, PLEN:], stacked(do_v, hd, s), NN).astype(BF16)
        gak_v[rows_of(s), cols] = (dot(
            ds_v[hd, s, PLEN:], stacked(q_v, hd, s), NN) * SCALING).astype(BF16)

    def block_rows(p):
        return pl.ds(pl.multiple_of(lax.rem(h + p, heads) * span, span), span)

    back_y, back_x, back_own = [], [], []
    for b, (w, hd, count) in enumerate(outward):
        back_y.append([
            remote(y_out[b].at[i], y_in[b].at[i], by_send.at[b, i], by_recv.at[b, i], dp=near[i])
            for i in range(len(near))
        ])
        dst = (gpk_out, gpv_out)[w].at[:, columns_at(h, hd, count)]
        back_x.append([
            remote(x_out[b].at[block_rows(p)], dst, bx_send.at[b, p - 1], bx_recv.at[b, p - 1],
                   head=peers[p - 1]) for p in order
        ])
        back_own.append(pltpu.make_async_copy(x_out[b].at[mine], dst, bx_own.at[b]))

    def summed(b, o):
        total = None
        for s in range(slots):
            term = part[b][s] * picks[s, o]
            total = term if total is None else total + term
        return total

    def send_back(b):
        for i, o in enumerate(offsets):
            y_out[b][i] = summed(b, o).astype(BF16)
            back_y[b][i].start()
        own[b][...] = summed(b, 0)

    def take_back(b):
        for copy in back_y[b]:
            copy.wait_recv()
        for p, copy in zip(order + [0], back_x[b] + [back_own[b]]):
            at = block_rows(p)
            total = own[b][at]
            for i in range(len(near)):
                total = total + y_in[b][i, at].astype(F32)
            x_out[b][at] = total.astype(BF16)
            copy.start()

    def each_slot(work, hd):
        for s in range(slots):
            work(hd, s)

    count_in = len(inward)
    exchange(0)
    forward(0, 0)
    for b in range(1, count_in):
        exchange(b)
    forward(1, 0)
    for b in range(2):
        for p in order:
            forward(b, p)
    for b in range(2, count_in):
        forward_whole(b)
    for load in loads:
        load.wait()
    picks = {
        (s, o): jnp.where(relative(s) == MAX_SPREAD + o, 1.0, 0.0).astype(F32)
        for s in range(slots) for o in offsets + [0]
    }
    for hd in range(kvh):
        each_slot(answer_scores, hd)

    arrived(0)
    for hd in range(kvh):
        each_slot(probabilities, hd)
    send_back(0)
    for hd in range(kvh):
        arrived(1 + hd)
        each_slot(gradients, hd)
        send_back(1 + hd)

    for hd in range(kvh - 1):
        each_slot(row_outputs, hd)
    for b in range(len(outward) - 1):
        take_back(b)
    row_outputs(kvh - 1, 0)
    take_back(len(outward) - 1)
    for s in range(1, slots):
        row_outputs(kvh - 1, s)

    for copy in [*x_in.values(), *y_in_copies.values()]:
        copy.wait_send()
    for b in range(len(outward)):
        for copy in back_y[b]:
            copy.wait_send()
        for copy in back_x[b]:
            copy.wait()
        back_own[b].wait()


def finish(o, dq, gak, gav, gpk, gpv, o_out, dq_out, gak_out, gav_out, gpk_out, gpv_out,
           wide_k, wide_v, sem):
    copies = [
        pltpu.make_async_copy(src, dst, sem.at[i])
        for i, (src, dst) in enumerate(
            [(o, o_out), (dq, dq_out), (gak, gak_out), (gav, gav_out),
             (wide_k, gpk_out.at[0]), (wide_v, gpv_out.at[0])])
    ]
    for copy in copies[:4]:
        copy.start()
    wide_k[...] = gpk[...].astype(F32)
    copies[4].start()
    wide_v[...] = gpv[...].astype(F32)
    copies[5].start()
    for copy in copies:
        copy.wait()


def on_device(queries, answer_keys, answer_values, prompt_keys, prompt_values,
              output_gradient, prompt_len, response_len, response_prompt):
    devices, heads = lax.axis_size("dp"), lax.axis_size("head")
    slots = response_len.shape[0]
    token_rows, q_width = queries.shape
    rows = token_rows // slots
    width = answer_keys.shape[1]
    kvh = width // HEAD_SIZE
    group = q_width // width
    lanes = group * rows
    span, full = prompt_keys.shape[1:]
    dma = pltpu.SemaphoreType.DMA
    anywhere = pl.BlockSpec(memory_space=pl.ANY)
    hbm = pl.BlockSpec(memory_space=pltpu.HBM)
    vmem = pl.BlockSpec(memory_space=pltpu.VMEM)
    vm, sm = pltpu.VMEM, pltpu.SMEM
    wide = vm((token_rows, q_width), BF16)
    narrow = vm((token_rows, width), BF16)
    square = (PLEN + rows, lanes)
    scratch = [
        sm(prompt_len.shape, jnp.int32), sm(response_len.shape, jnp.int32),
        sm(response_prompt.shape, jnp.int32),
        wide, wide, narrow, narrow, vm((kvh, slots) + square, F32),
        vm((kvh, slots) + square, BF16), vm((kvh, slots) + square, BF16),
        vm((span, full), BF16), vm((span, full), BF16),
        vm((kvh, slots, rows, lanes), F32), vm((kvh, slots, rows, lanes), F32),
    ]
    shapes = [(PLEN, width)] + [(PLEN, HEAD_SIZE)] * kvh
    scratch += [vm((REACH,) + shape, BF16) for shape in shapes]
    for lead, kind in [((slots,), F32), ((REACH - 1,), BF16), ((REACH - 1,), BF16),
                       ((), F32), ((), BF16)]:
        scratch += [vm(lead + shape, kind) for shape in shapes]
    scratch += [
        dma((7,)),
        dma((kvh + 1, heads - 1)), dma((kvh + 1, heads - 1)), dma((2,)),
        dma((kvh + 1, heads, REACH - 1)), dma((kvh + 1, heads, REACH - 1)),
        dma((kvh + 1, REACH - 1)), dma((kvh + 1, REACH - 1)),
        dma((kvh + 1, heads - 1)), dma((kvh + 1, heads - 1)), dma((kvh + 1,)),
    ]
    sds = jax.ShapeDtypeStruct
    rows_out = [
        sds((token_rows, q_width), BF16), sds((token_rows, q_width), BF16),
        sds((token_rows, width), BF16), sds((token_rows, width), BF16),
    ]
    results = pl.pallas_call(
        functools.partial(kernel, (devices, heads, slots, rows, kvh, group)),
        out_shape=rows_out + [sds((span, full), BF16), sds((span, full), BF16)],
        in_specs=[hbm] * 9,
        out_specs=[vmem] * 4 + [anywhere] * 2,
        scratch_shapes=scratch,
        compiler_params=pltpu.CompilerParams(
            collective_id=0, has_side_effects=True, vmem_limit_bytes=48 * 1024 * 1024),
    )(*[pltpu.with_memory_space_constraint(x, pltpu.HBM) for x in (
        prompt_len, response_len, response_prompt, queries, output_gradient,
        answer_keys, answer_values, prompt_keys.reshape(span, full),
        prompt_values.reshape(span, full))])
    return pl.pallas_call(
        finish,
        out_shape=rows_out + [sds((1, span, full), F32), sds((1, span, full), F32)],
        in_specs=[vmem] * 6,
        out_specs=[anywhere] * 6,
        scratch_shapes=[vm((span, full), F32), vm((span, full), F32), dma((6,))],
        compiler_params=pltpu.CompilerParams(vmem_limit_bytes=4 * 1024 * 1024),
    )(*[pltpu.with_memory_space_constraint(x, pltpu.VMEM) for x in results])


def solution(mesh):
    in_specs = (
        P("dp", "head"),
        P("dp", "head"),
        P("dp", "head"),
        P("dp", "head", None),
        P("dp", "head", None),
        P("dp", "head"),
        P(),
        P("dp"),
        P("dp"),
    )
    out_specs = (
        P("dp", "head"),
        P("dp", "head"),
        P("dp", "head"),
        P("dp", "head"),
        P("dp", "head", None),
        P("dp", "head", None),
    )
    return jax.shard_map(
        on_device, mesh=mesh, in_specs=in_specs, out_specs=out_specs, check_vma=False
    )
```

time: 40 us -> 42 us (1.050)
  Pallas kernels: 39.2 us -> 41.3 us
    pallas_call x1, Pallas kernels: 37.6 us -> 39.6 us  [on_device(): pl.pallas_call(functools.partial(kernel, (devices, heads, slots, rows, kv...]
where the time goes in v9:
time: 42 us; the launch traced here: 41.9 us
  Pallas kernels  41.3 us (98%)
  between operations  0.64 us (2%)
    pallas_call x1, Pallas kernels, on_device(): pl.pallas_call(functools.partial(kernel, (devices, heads, slots, rows, kv...  39.6 us
    pallas_call x1, Pallas kernels, on_device(): pl.pallas_call(finish, out_shape=rows_out + [sds((1, span, full), F32), s...  1.62 us

profile of v9, /device:TPU:1, one launch (start us, length us, event | category | flops | bytes accessed | tf_op | source)
XLA Modules:
  0.0 41.9 jit_solution(10889465254091368849)
XLA Ops:
  0.6 39.6 %shard_map.136 = (bf16[256,2048]{1,0:T(8,128)(2,1)S(1)}, bf16[256,2048]{1,0:T(8,128)(2,1)S(1)}, bf16[256,256]{1,0:T(8,128)(2,1)S(1)}, bf16[256,256]{1,0:T(8,128)...) custom-call(s32[64]{0:T(128)} %refs_0_.1, s32[4]{0:T(128)} %refs_1_.1, s32[4]{0:T(128)} %refs_2_.1, ...), custom_call_target="tpu_custom_call" | custom-call | tf_op jit(solution)/shard_map/pallas_call | solution.py:349
  40.3 1.6 %shard_map.137 = (bf16[256,2048]{1,0:T(8,128)(2,1)}, bf16[256,2048]{1,0:T(8,128)(2,1)}, bf16[256,256]{1,0:T(8,128)(2,1)}, bf16[256,256]{1,0:T(8,128)(2,1)}, f32[...) custom-call(bf16[256,2048]{1,0:T(8,128)(2,1)S(1)} %get-tuple-element.12.o, bf16[256,2048]{1,0:T(8,128)(2,1)S(1)} %get-tuple-element.13.dq, ...), custom_call_target="tpu_custom_call" | custom-call | tf_op jit(solution)/shard_map/pallas_call | solution.py:361

commit v10 on v6

--- a/solution.py
+++ b/solution.py
@@ -36,13 +36,13 @@
     (plen_hbm, rlen_hbm, rprompt_hbm, q_hbm, do_hbm, ak_hbm, av_hbm, pk_hbm, pv_hbm,
      o_v, dq_v, gak_v, gav_v, gpk_out, gpv_out,
      plen_ref, rlen_ref, rprompt_ref,
-     q_v, do_v, ak_v, av_v, p_v, w_v, ds_v, pk_v, pv_v, st_v, gt_v) = refs[:29]
-    kv, refs = refs[29:29 + len(bundles)], refs[29 + len(bundles):]
+     q_v, do_v, ak_v, av_v, p_v, w_v, ds_v, pk_v, pv_v, s_v) = refs[:28]
+    kv, refs = refs[28:28 + len(bundles)], refs[28 + len(bundles):]
     (part, y_out, y_in, own, x_out) = [
         dict(zip(pairs, refs[i * len(pairs):(i + 1) * len(pairs)])) for i in range(5)
     ]
     (in_sem, x_send, x_recv, x_own, y_send, y_recv,
-     by_send, by_recv, bx_send, bx_recv, bx_own, bl_send, bl_recv) = refs[5 * len(pairs):]
+     by_send, by_recv, bx_send, bx_recv, bx_own) = refs[5 * len(pairs):]
 
     me = lax.axis_index("dp")
     h = lax.axis_index("head")
@@ -138,40 +138,44 @@
     def answer_part(hd, w, s):
         return (ak_v, av_v)[w][rows_of(s), hd * HEAD_SIZE:(hd + 1) * HEAD_SIZE]
 
-    def answer_scores(hd, s):
-        seen = lax.broadcasted_iota(jnp.int32, (rows, lanes), 0) <= (
-            lax.broadcasted_iota(jnp.int32, (rows, lanes), 1) & (rows - 1))
-        scores = dot(answer_part(hd, 0, s), stacked(q_v, hd, s), NT)
-        st_v[hd, s] = jnp.where(seen, scores, -jnp.inf)
-        gt_v[hd, s] = dot(answer_part(hd, 1, s), stacked(do_v, hd, s), NT)
+    def everything(hd, w, s):
+        return jnp.concatenate([prompt_part(hd, w, s), answer_part(hd, w, s)], axis=0)
+
+    lane_chunks = [slice(c, c + 128) for c in range(0, lanes, 128)]
+    row_chunks = [slice(r, r + rows) for r in range(0, PLEN + rows, rows)]
 
     def probabilities(hd, s):
         psize = plen_ref[rprompt_ref[s]]
         rlen = rlen_ref[s]
-        live = ((lax.broadcasted_iota(jnp.int32, (1, lanes), 1) & (rows - 1)) < rlen).astype(F32)
-        seen = lax.broadcasted_iota(jnp.int32, (PLEN, lanes), 0) < psize
-        scores = dot(prompt_part(hd, 0, s), stacked(q_v, hd, s), NT)
-        masked = jnp.concatenate([jnp.where(seen, scores, -jnp.inf), st_v[hd, s]], axis=0)
-        top = jnp.max(masked, axis=0, keepdims=True)
-        e = jnp.exp2((masked - top) * (SCALING * math.log2(math.e)))
-        prob = e * (live / jnp.sum(e, axis=0, keepdims=True))
-        p_v[s] = prob
-        weights = prob.astype(BF16)
-        w_v[hd, s] = weights
-        part[hd, 1][s] = dot(weights[:PLEN], stacked(do_v, hd, s), NN)
+        s_v[s] = dot(everything(hd, 0, s), stacked(q_v, hd, s), NT)
+        column = lax.broadcasted_iota(jnp.int32, (rows, 128), 1) & (rows - 1)
+        row = lax.broadcasted_iota(jnp.int32, (rows, 128), 0)
+        live = (column[:1] < rlen).astype(F32)
+        for at in lane_chunks:
+            masked = jnp.concatenate([
+                jnp.where(row < psize - r.start if r.start < PLEN else row <= column,
+                          s_v[s, r, at], -jnp.inf) for r in row_chunks], axis=0)
+            top = jnp.max(masked, axis=0, keepdims=True)
+            e = jnp.exp2((masked - top) * (SCALING * math.log2(math.e)))
+            prob = e * (live / jnp.sum(e, axis=0, keepdims=True))
+            p_v[s, :, at] = prob
+            w_v[hd, s, :, at] = prob.astype(BF16)
+        part[hd, 1][s] = dot(w_v[hd, s, :PLEN], stacked(do_v, hd, s), NN)
 
     def gradients(hd, s):
-        prob = p_v[s]
-        gprob = jnp.concatenate([
-            dot(prompt_part(hd, 1, s), stacked(do_v, hd, s), NT), gt_v[hd, s]], axis=0)
-        delta = jnp.sum(prob * gprob, axis=0, keepdims=True)
-        gscores = (prob * (gprob - delta)).astype(BF16)
-        ds_v[hd, s] = gscores
-        part[hd, 0][s] = dot(gscores[:PLEN], stacked(q_v, hd, s), NN) * SCALING
+        s_v[s] = dot(everything(hd, 1, s), stacked(do_v, hd, s), NT)
+        for at in lane_chunks:
+            delta = jnp.zeros((rows, 128), F32)
+            for r in row_chunks:
+                delta = delta + p_v[s, r, at] * s_v[s, r, at]
+            delta = jnp.sum(delta, axis=0, keepdims=True)
+            for r in row_chunks:
+                ds_v[hd, s, r, at] = (p_v[s, r, at] * (s_v[s, r, at] - delta)).astype(BF16)
+        part[hd, 0][s] = dot(ds_v[hd, s, :PLEN], stacked(q_v, hd, s), NN) * SCALING
 
     def row_outputs(hd, s):
-        keys_t = jnp.concatenate([prompt_part(hd, 0, s), answer_part(hd, 0, s)], axis=0).T
-        values_t = jnp.concatenate([prompt_part(hd, 1, s), answer_part(hd, 1, s)], axis=0).T
+        keys_t = everything(hd, 0, s).T
+        values_t = everything(hd, 1, s).T
         out = dot(values_t, w_v[hd, s], NN).astype(BF16).T
         dq = (dot(keys_t, ds_v[hd, s], NN) * SCALING).astype(BF16).T
         for g, col in enumerate(columns(hd)):
@@ -203,46 +207,31 @@
             x_out[pair].at[mine], dst.at[:, cols], bx_own.at[hd, w])
 
     last = kvh - 1, 0
-    back_last = {}
-    for p in range(heads):
-        at = pl.ds(pl.multiple_of(lax.rem(h + p, heads) * span, span), span)
-        for i in range(len(near)):
-            back_last[p, i] = remote(
-                y_out[last].at[i, at], y_in[last].at[i, at], bl_send.at[p, i],
-                bl_recv.at[p, i], dp=near[i])
 
     def block_rows(p):
         return pl.ds(pl.multiple_of(lax.rem(h + p, heads) * span, span), span)
 
     def send_back(pair):
-        for p in order + [0]:
-            at = block_rows(p)
-            terms = [part[pair][s, at] for s in range(slots)]
-            for i, o in enumerate(offsets + [0]):
+        for i, o in enumerate(offsets + [0]):
+            for r in row_chunks[:-1]:
                 total = None
                 for s in range(slots):
-                    term = terms[s] * picks[s, o]
+                    term = part[pair][s, r] * picks[s, o]
                     total = term if total is None else total + term
                 if o == 0:
-                    own[pair][at] = total
+                    own[pair][r] = total
                 else:
-                    y_out[pair][i, at] = total.astype(BF16)
-                    if pair == last:
-                        back_last[p, i].start()
-        if pair != last:
-            for copy in back_y[pair]:
-                copy.start()
+                    y_out[pair][i, r] = total.astype(BF16)
+            if o != 0:
+                back_y[pair][i].start()
 
     def take_back(pair):
-        if pair != last:
-            for copy in back_y[pair]:
-                copy.wait_recv()
+        for copy in back_y[pair]:
+            copy.wait_recv()
         for p, copy in zip(order + [0], back_x[pair] + [back_own[pair]]):
             at = block_rows(p)
             total = own[pair][at]
             for i in range(len(near)):
-                if pair == last:
-                    back_last[p, i].wait_recv()
                 total = total + y_in[pair][i, at].astype(F32)
             x_out[pair][at] = total.astype(BF16)
             copy.start()
@@ -257,18 +246,15 @@
         exchange(*pair)
     for b in range(1, len(bundles)):
         forward(b, 0)
+    for b in range(len(bundles)):
+        for p in order:
+            forward(b, p)
     for load in loads:
         load.wait()
     picks = {
         (s, o): jnp.where(relative(s) == MAX_SPREAD + o, 1.0, 0.0).astype(F32)
         for s in range(slots) for o in offsets + [0]
     }
-    each_slot(answer_scores, 0)
-    for b in range(len(bundles)):
-        for p in order:
-            forward(b, p)
-    for hd in range(1, kvh):
-        each_slot(answer_scores, hd)
 
     for hd in range(kvh):
         arrived(hd + 1 if hd > 0 else 0)
@@ -292,13 +278,12 @@
     for pair in pairs:
         for p in order:
             x_in[(*pair, p)].wait_send()
-        if pair != last:
-            for copy in back_y[pair]:
-                copy.wait_send()
+        for copy in back_y[pair]:
+            copy.wait_send()
         for copy in back_x[pair]:
             copy.wait()
         back_own[pair].wait()
-    for copy in [*y_in_copies.values(), *back_last.values()]:
+    for copy in y_in_copies.values():
         copy.wait_send()
 
 
@@ -347,7 +332,7 @@
         wide, wide, narrow, narrow, vm((slots,) + square, F32),
         vm((kvh, slots) + square, BF16), vm((kvh, slots) + square, BF16),
         vm((span, full), BF16), vm((span, full), BF16),
-        vm((kvh, slots, rows, lanes), F32), vm((kvh, slots, rows, lanes), F32),
+        vm((slots,) + square, F32),
     ]
     scratch += [vm((REACH, count) + block, BF16) for count in bundle]
     for shape in [vm((slots,) + block, F32), vm((REACH - 1,) + block, BF16),
@@ -359,7 +344,6 @@
         dma((kvh + 1, heads, REACH - 1)), dma((kvh + 1, heads, REACH - 1)),
         dma((kvh, 2, REACH - 1)), dma((kvh, 2, REACH - 1)),
         dma((kvh, 2, heads - 1)), dma((kvh, 2, heads - 1)), dma((kvh, 2)),
-        dma((heads, REACH - 1)), dma((heads, REACH - 1)),
     ]
     sds = jax.ShapeDtypeStruct
     rows_out = [

time: 40 us -> 39.9 us (level)
  no operation moved by 1% of the time
where the time goes in v10:
time: 39.9 us; the launch traced here: 39.8 us
  Pallas kernels  39.1 us (98%)
  between operations  0.64 us (2%)
    pallas_call x1, Pallas kernels, on_device(): pl.pallas_call(functools.partial(kernel, (devices, heads, slots, rows, kv...  37.5 us
    pallas_call x1, Pallas kernels, on_device(): pl.pallas_call(finish, out_shape=rows_out + [sds((1, span, full), F32), s...  1.62 us

profile of v10, /device:TPU:1, one launch (start us, length us, event | category | flops | bytes accessed | tf_op | source)
XLA Modules:
  0.0 39.8 jit_solution(14544855541410811177)
XLA Ops:
  0.6 37.5 %shard_map.136 = (bf16[256,2048]{1,0:T(8,128)(2,1)S(1)}, bf16[256,2048]{1,0:T(8,128)(2,1)S(1)}, bf16[256,256]{1,0:T(8,128)(2,1)S(1)}, bf16[256,256]{1,0:T(8,128)...) custom-call(s32[64]{0:T(128)} %refs_0_.1, s32[4]{0:T(128)} %refs_1_.1, s32[4]{0:T(128)} %refs_2_.1, ...), custom_call_target="tpu_custom_call" | custom-call | tf_op jit(solution)/shard_map/pallas_call | solution.py:353
  38.2 1.6 %shard_map.137 = (bf16[256,2048]{1,0:T(8,128)(2,1)}, bf16[256,2048]{1,0:T(8,128)(2,1)}, bf16[256,256]{1,0:T(8,128)(2,1)}, bf16[256,256]{1,0:T(8,128)(2,1)}, f32[...) custom-call(bf16[256,2048]{1,0:T(8,128)(2,1)S(1)} %get-tuple-element.12.o, bf16[256,2048]{1,0:T(8,128)(2,1)S(1)} %get-tuple-element.13.dq, ...), custom_call_target="tpu_custom_call" | custom-call | tf_op jit(solution)/shard_map/pallas_call | solution.py:365

commit v11 on v5

--- a/solution.py
+++ b/solution.py
@@ -211,13 +211,28 @@
             total = term if total is None else total + term
         return total
 
+    last = kvh - 1, 0
+    core = lax.rem(me, 2)
+    sibling = me + 1 - 2 * core
+    direct_to = lax.rem(me + devices - 2 + 4 * core, devices)
+    relay_to = lax.rem(me + devices + 2 - 4 * core, devices)
     back_y, back_x, back_own = {}, {}, {}
     for hd, w in pairs:
         pair = hd, w
-        back_y[pair] = [
-            remote(y_out[pair].at[i], y_in[pair].at[i], by_send.at[hd, w, i],
-                   by_recv.at[hd, w, i], dp=near[i]) for i in range(len(near))
-        ]
+        if pair == last:
+            back_y[pair] = [
+                remote(y_out[pair].at[i], y_in[pair].at[i], by_send.at[hd, w, i],
+                       by_recv.at[hd, w, i], dp=near[i]) for i in range(len(near))
+            ]
+        else:
+            back_y[pair] = [
+                remote(y_out[pair].at[core], y_in[pair].at[core], by_send.at[hd, w, 0],
+                       by_recv.at[hd, w, core], dp=direct_to),
+                remote(y_out[pair].at[1 - core], y_in[pair].at[1 - core], by_send.at[hd, w, 1],
+                       by_recv.at[hd, w, 1 - core], dp=relay_to),
+                remote(y_out[pair].at[2:4], y_in[pair].at[2:4], by_send.at[hd, w, 2],
+                       by_recv.at[hd, w, 2], dp=sibling),
+            ]
         dst = (gpk_out, gpv_out)[w]
         cols = pl.ds(pl.multiple_of(h * width + hd * HEAD_SIZE, HEAD_SIZE), HEAD_SIZE)
         back_x[pair] = []
@@ -231,46 +246,65 @@
             x_out[pair].at[mine], dst.at[:, cols], bx_own.at[hd, w])
 
     def send_back(pair):
-        for i, o in enumerate(offsets):
-            y_out[pair][i] = summed(pair, MAX_SPREAD + o).astype(BF16)
-            back_y[pair][i].start()
+        if pair == last:
+            for i, o in enumerate(offsets):
+                y_out[pair][i] = summed(pair, MAX_SPREAD + o).astype(BF16)
+                back_y[pair][i].start()
+        else:
+            for i in (2, 3):
+                y_out[pair][i] = summed(pair, MAX_SPREAD + offsets[i]).astype(BF16)
+            back_y[pair][2].start()
+            y_out[pair][core] = summed(pair, 4 * core).astype(BF16)
+            back_y[pair][0].start()
         own[pair][...] = summed(pair, MAX_SPREAD)
 
+    def relay_back(pair):
+        carry = summed(pair, 4 - 4 * core)
+        back_y[pair][2].wait_recv()
+        y_out[pair][1 - core] = (carry + y_in[pair][3 - core].astype(F32)).astype(BF16)
+        back_y[pair][1].start()
+
     def take_back(pair):
-        for copy in back_y[pair]:
-            copy.wait_recv()
+        if pair == last:
+            for copy in back_y[pair]:
+                copy.wait_recv()
+            came = [0, 1, 2, 3]
+        else:
+            for copy in back_y[pair][:2]:
+                copy.wait_recv()
+            came = [0, 1, 2 + core]
         for p, copy in zip(order + [0], back_x[pair] + [back_own[pair]]):
             at = pl.ds(pl.multiple_of(lax.rem(h + p, heads) * span, span), span)
             total = own[pair][at]
-            for i in range(len(near)):
+            for i in came:
                 total = total + y_in[pair][i, at].astype(F32)
             x_out[pair][at] = total.astype(BF16)
             copy.start()
 
     def each_slot(work, hd, at={}):
         for s in range(slots):
+            for what, *args in at.get(s, ()):
+                what(*args)
             work(hd, s)
-            for pair in at.get(s, ()):
-                take_back(pair)
-
+
+    half = slots // 2
     for hd in range(kvh):
-        if hd == 0:
-            arrived(0)
-        else:
-            arrived(hd + 1)
-        each_slot(probabilities, hd)
+        arrived(hd + 1 if hd > 0 else 0)
+        each_slot(probabilities, hd, {half: [(relay_back, (hd - 1, 0))]} if hd > 0 else {})
         send_back((hd, 1))
         if hd == 0:
             arrived(1)
-        each_slot(gradients, hd)
+        each_slot(gradients, hd, {half: [(relay_back, (hd, 1))]})
         send_back((hd, 0))
 
     end = kvh - 1
     for hd in range(kvh):
         if hd < end:
-            each_slot(row_outputs, hd, {slots - 1: [(hd, 1), (hd, 0)]})
+            each_slot(row_outputs, hd)
+            take_back((hd, 1))
+            take_back((hd, 0))
         else:
-            each_slot(row_outputs, hd, {0: [(end, 1)], slots // 2: [(end, 0)]})
+            each_slot(row_outputs, hd, {1: [(take_back, (end, 1)), (take_back, last)]})
 
     for pair in pairs:
         for p in order:

time: 39.3 us -> 39.1 us (level)
  no operation moved by 1% of the time
where the time goes in v11:
time: 39.1 us; the launch traced here: 39 us
  Pallas kernels  38.3 us (98%)
  between operations  0.64 us (2%)
    pallas_call x1, Pallas kernels, on_device(): pl.pallas_call(functools.partial(kernel, (devices, heads, slots, rows, kv...  36.7 us
    pallas_call x1, Pallas kernels, on_device(): pl.pallas_call(finish, out_shape=rows_out + [sds((1, span, full), F32), s...  1.62 us

profile of v11, /device:TPU:1, one launch (start us, length us, event | category | flops | bytes accessed | tf_op | source)
XLA Modules:
  0.0 39.0 jit_solution(13306971285325344739)
XLA Ops:
  0.6 36.7 %shard_map.136 = (bf16[256,2048]{1,0:T(8,128)(2,1)S(1)}, bf16[256,2048]{1,0:T(8,128)(2,1)S(1)}, bf16[256,256]{1,0:T(8,128)(2,1)S(1)}, bf16[256,256]{1,0:T(8,128)...) custom-call(s32[64]{0:T(128)} %refs_0_.1, s32[4]{0:T(128)} %refs_1_.1, s32[4]{0:T(128)} %refs_2_.1, ...), custom_call_target="tpu_custom_call" | custom-call | tf_op jit(solution)/shard_map/pallas_call | solution.py:383
  37.4 1.6 %shard_map.137 = (bf16[256,2048]{1,0:T(8,128)(2,1)}, bf16[256,2048]{1,0:T(8,128)(2,1)}, bf16[256,256]{1,0:T(8,128)(2,1)}, bf16[256,256]{1,0:T(8,128)(2,1)}, f32[...) custom-call(bf16[256,2048]{1,0:T(8,128)(2,1)S(1)} %get-tuple-element.12.o, bf16[256,2048]{1,0:T(8,128)(2,1)S(1)} %get-tuple-element.13.dq, ...), custom_call_target="tpu_custom_call" | custom-call | tf_op jit(solution)/shard_map/pallas_call | solution.py:395

commit v12 on v11

--- a/solution.py
+++ b/solution.py
@@ -109,14 +109,36 @@
                 x_in[(*pair, piece)].wait_recv()
         source = lax.rem(h + heads - piece, heads)
         at = pl.ds(pl.multiple_of(source * span, span), span)
-        for i, o in enumerate(offsets):
+        for i, o in enumerate(offsets[:2] if b >= 2 else offsets):
             copy = remote(
                 kv[b].at[MAX_SPREAD, :, at], kv[b].at[MAX_SPREAD - o, :, at],
                 y_send.at[b, piece, i], y_recv.at[b, piece, i], dp=near[i])
             y_in_copies[b, piece, i] = copy
             copy.start()
 
+    core = lax.rem(me, 2)
+    sibling = me + 1 - 2 * core
+
+    def to_sibling(b):
+        y_in_copies[b, 0, 2] = remote(
+            kv[b].at[MAX_SPREAD], kv[b].at[1 + 2 * core], y_send.at[b, 0, 2], y_recv.at[b, 0, 2],
+            dp=sibling)
+        y_in_copies[b, 0, 2].start()
+
+    def relay_in(b):
+        for piece in range(heads):
+            for i in range(2):
+                y_in_copies[b, piece, i].wait_recv()
+        y_in_copies[b, 0, 3] = remote(
+            kv[b].at[4 - 4 * core], kv[b].at[3 - 2 * core], y_send.at[b, 0, 3],
+            y_recv.at[b, 0, 3], dp=sibling)
+        y_in_copies[b, 0, 3].start()
+
     def arrived(b):
+        if b >= 2:
+            y_in_copies[b, 0, 2].wait_recv()
+            y_in_copies[b, 0, 3].wait_recv()
+            return
         for piece in range(heads):
             for i in range(len(near)):
                 y_in_copies[b, piece, i].wait_recv()
@@ -130,6 +152,8 @@
     for b in range(len(bundles)):
         for p in order:
             forward(b, p)
+        if b >= 2:
+            to_sibling(b)
     for load in loads:
         load.wait()
 
@@ -212,8 +236,6 @@
         return total
 
     last = kvh - 1, 0
-    core = lax.rem(me, 2)
-    sibling = me + 1 - 2 * core
     direct_to = lax.rem(me + devices - 2 + 4 * core, devices)
     relay_to = lax.rem(me + devices + 2 - 4 * core, devices)
     back_y, back_x, back_own = {}, {}, {}
@@ -294,7 +316,10 @@
         send_back((hd, 1))
         if hd == 0:
             arrived(1)
-        each_slot(gradients, hd, {half: [(relay_back, (hd, 1))]})
+        at = {half: [(relay_back, (hd, 1))]}
+        if hd + 1 < kvh:
+            at[slots - 1] = at.get(slots - 1, []) + [(relay_in, hd + 2)]
+        each_slot(gradients, hd, at)
         send_back((hd, 0))
 
     end = kvh - 1

time: 39.1 us -> 39.1 us (level)
  no operation moved by 1% of the time
where the time goes in v12:
time: 39.1 us; the launch traced here: 39 us
  Pallas kernels  38.4 us (98%)
  between operations  0.64 us (2%)
    pallas_call x1, Pallas kernels, on_device(): pl.pallas_call(functools.partial(kernel, (devices, heads, slots, rows, kv...  36.8 us
    pallas_call x1, Pallas kernels, on_device(): pl.pallas_call(finish, out_shape=rows_out + [sds((1, span, full), F32), s...  1.62 us

profile of v12, /device:TPU:1, one launch (start us, length us, event | category | flops | bytes accessed | tf_op | source)
XLA Modules:
  0.0 39.0 jit_solution(10221852749893835059)
XLA Ops:
  0.6 36.8 %shard_map.136 = (bf16[256,2048]{1,0:T(8,128)(2,1)S(1)}, bf16[256,2048]{1,0:T(8,128)(2,1)S(1)}, bf16[256,256]{1,0:T(8,128)(2,1)S(1)}, bf16[256,256]{1,0:T(8,128)...) custom-call(s32[64]{0:T(128)} %refs_0_.1, s32[4]{0:T(128)} %refs_1_.1, s32[4]{0:T(128)} %refs_2_.1, ...), custom_call_target="tpu_custom_call" | custom-call | tf_op jit(solution)/shard_map/pallas_call | solution.py:408
  37.4 1.6 %shard_map.137 = (bf16[256,2048]{1,0:T(8,128)(2,1)}, bf16[256,2048]{1,0:T(8,128)(2,1)}, bf16[256,256]{1,0:T(8,128)(2,1)}, bf16[256,256]{1,0:T(8,128)(2,1)}, f32[...) custom-call(bf16[256,2048]{1,0:T(8,128)(2,1)S(1)} %get-tuple-element.12.o, bf16[256,2048]{1,0:T(8,128)(2,1)S(1)} %get-tuple-element.13.dq, ...), custom_call_target="tpu_custom_call" | custom-call | tf_op jit(solution)/shard_map/pallas_call | solution.py:420

commit v13 on v11

--- a/solution.py
+++ b/solution.py
@@ -30,7 +30,7 @@
 def kernel(sizes, *refs):
     devices, heads, slots, rows, kvh, group = sizes
     pairs = [(hd, w) for hd in range(kvh) for w in range(2)]
-    bundles = [[(0, 0)], [(0, 1)]] + [[(hd, 0), (hd, 1)] for hd in range(1, kvh)]
+    bundles = [[pair] for pair in pairs]
     place = {pair: (b, j) for b, bundle in enumerate(bundles) for j, pair in enumerate(bundle)}
     refs = list(refs)
     (plen_hbm, rlen_hbm, rprompt_hbm, q_hbm, do_hbm, ak_hbm, av_hbm, pk_hbm, pv_hbm,
@@ -289,11 +289,10 @@
 
     half = slots // 2
     for hd in range(kvh):
-        arrived(hd + 1 if hd > 0 else 0)
+        arrived(2 * hd)
         each_slot(probabilities, hd, {half: [(relay_back, (hd - 1, 0))]} if hd > 0 else {})
         send_back((hd, 1))
-        if hd == 0:
-            arrived(1)
+        arrived(2 * hd + 1)
         each_slot(gradients, hd, {half: [(relay_back, (hd, 1))]})
         send_back((hd, 0))
 
@@ -356,7 +355,7 @@
     wide = vm((token_rows, q_width), BF16)
     narrow = vm((token_rows, width), BF16)
     square = (PLEN + rows, lanes)
-    bundle = [1, 1] + [2] * (kvh - 1)
+    bundle = [1] * (2 * kvh)
     scratch = [
         sm(prompt_len.shape, jnp.int32), sm(response_len.shape, jnp.int32),
         sm(response_prompt.shape, jnp.int32),
@@ -371,7 +370,7 @@
     scratch += [
         dma((7,)),
         dma((kvh, 2, heads - 1)), dma((kvh, 2, heads - 1)), dma((2,)),
-        dma((kvh + 1, heads, REACH - 1)), dma((kvh + 1, heads, REACH - 1)),
+        dma((2 * kvh, heads, REACH - 1)), dma((2 * kvh, heads, REACH - 1)),
         dma((kvh, 2, REACH - 1)), dma((kvh, 2, REACH - 1)),
         dma((kvh, 2, heads - 1)), dma((kvh, 2, heads - 1)), dma((kvh, 2)),
     ]

time: 39.1 us -> 39.4 us (level)
  no operation moved by 1% of the time
where the time goes in v13:
time: 39.4 us; the launch traced here: 39.3 us
  Pallas kernels  38.6 us (98%)
  between operations  0.64 us (2%)
    pallas_call x1, Pallas kernels, on_device(): pl.pallas_call(functools.partial(kernel, (devices, heads, slots, rows, kv...  37 us
    pallas_call x1, Pallas kernels, on_device(): pl.pallas_call(finish, out_shape=rows_out + [sds((1, span, full), F32), s...  1.62 us

profile of v13, /device:TPU:1, one launch (start us, length us, event | category | flops | bytes accessed | tf_op | source)
XLA Modules:
  0.0 39.3 jit_solution(6879337948141934637)
XLA Ops:
  0.6 37.0 %shard_map.136 = (bf16[256,2048]{1,0:T(8,128)(2,1)S(1)}, bf16[256,2048]{1,0:T(8,128)(2,1)S(1)}, bf16[256,256]{1,0:T(8,128)(2,1)S(1)}, bf16[256,256]{1,0:T(8,128)...) custom-call(s32[64]{0:T(128)} %refs_0_.1, s32[4]{0:T(128)} %refs_1_.1, s32[4]{0:T(128)} %refs_2_.1, ...), custom_call_target="tpu_custom_call" | custom-call | tf_op jit(solution)/shard_map/pallas_call | solution.py:382
  37.7 1.6 %shard_map.137 = (bf16[256,2048]{1,0:T(8,128)(2,1)}, bf16[256,2048]{1,0:T(8,128)(2,1)}, bf16[256,256]{1,0:T(8,128)(2,1)}, bf16[256,256]{1,0:T(8,128)(2,1)}, f32[...) custom-call(bf16[256,2048]{1,0:T(8,128)(2,1)S(1)} %get-tuple-element.12.o, bf16[256,2048]{1,0:T(8,128)(2,1)S(1)} %get-tuple-element.13.dq, ...), custom_call_target="tpu_custom_call" | custom-call | tf_op jit(solution)/shard_map/pallas_call | solution.py:394
